TPU v7x, 512 devices: a whole 4x8x8 slice. The times are simulated.
512 devices in a mesh: prow: 32 (over x, z), pcol: 16 (over y, core).
Axes of the slice: x: 4, y: 8, z: 8, core: 2. Of those that a mesh axis runs over, the one named last changes fastest.
Arguments:
- inverse_block: float32 [4, 32, 128, 8, 16, 128], P(None, 'prow', None, None, 'pcol'), may hold values from -6 to 6
- panel_first: float32 [4, 32, 256, 128], P(None, 'prow', 'pcol'), may hold values from -0.046875 to 0.046875
- panel_second: float32 [4, 32, 256, 128], P(None, 'prow', 'pcol'), may hold values from -0.046875 to 0.046875
- coupling: float32 [256, 256], P('prow'), may hold values from -0.375 to 0.375
- dinv_first: float32 [256, 256], replicated, may hold values from -6 to 6
- dinv_second: float32 [256, 256], replicated, may hold values from -6 to 6
- struct_first: int32 [128], replicated, may hold values 0 or 1
- struct_second: int32 [128], replicated, may hold values 0 or 1
Outputs:
- row_first: float32 [8, 16, 256, 128], P(None, 'pcol', 'prow')
- own_first: float32 [256, 256], replicated
- row_second: float32 [8, 16, 256, 128], P(None, 'pcol', 'prow')
- cross: float32 [256, 256], replicated
- own_second: float32 [256, 256], replicated
Inputs may be any that keep to these rules, and one draw needn't show every extreme that they name: `struct_first`: 1 marks a block that lies in the supernode's structure, 0 one that does not. `struct_second`: 1 marks a block that lies in the supernode's structure, 0 one that does not.
All inputs are finite; a program needn't handle non-finite values.
Results may differ from a plain program's by a relative error of at most 0.000084.
Values sent between devices are 32-bit elements; how exact they have to be, the bound alone decides.
A program may use at most 64 MiB of HBM per device.

v0:
```python
import jax
import jax.numpy as jnp
from jax import lax
from jax.sharding import PartitionSpec as P


def body(
    inverse_block,
    panel_first,
    panel_second,
    coupling,
    dinv_first,
    dinv_second,
    struct_first,
    struct_second,
):
    highest = lax.Precision.HIGHEST
    rows = lax.axis_size("prow")
    cols = lax.axis_size("pcol")
    prow_index = lax.axis_index("prow")
    pcol_index = lax.axis_index("pcol")
    ratio = rows // cols
    row_blocks = inverse_block.shape[0]
    blk = inverse_block.shape[2]
    col_blocks = inverse_block.shape[3]
    slab = coupling.shape[0]
    width = coupling.shape[1]
    local = inverse_block.reshape(row_blocks, blk, col_blocks, blk)
    diagonal = (prow_index % cols == pcol_index).astype(jnp.float32)

    def row_mask(struct):
        table = struct.astype(jnp.float32).reshape(row_blocks, rows)
        return lax.dynamic_slice_in_dim(table, prow_index, 1, 1)[:, :, None]

    def col_mask(struct):
        table = struct.astype(jnp.float32).reshape(col_blocks, cols)
        return lax.dynamic_slice_in_dim(table, pcol_index, 1, 1)[:, :, None]

    def matching(full):
        grouped = full.reshape(row_blocks, ratio, width, blk)
        return lax.dynamic_slice_in_dim(grouped, prow_index // cols, 1, 1)[:, 0]

    def my_rows(full):
        return lax.dynamic_slice_in_dim(full, prow_index * slab, slab, 1)

    def product(panel, mask):
        return jnp.einsum("rwx,rxcy->cwy", panel * mask, local, precision=highest)

    panel_a = lax.all_gather(panel_first, "pcol", axis=2, tiled=True)[:, 0]
    panel_b = lax.all_gather(panel_second, "pcol", axis=2, tiled=True)[:, 0]
    coupling_full = lax.all_gather(coupling, "prow", axis=0, tiled=True)
    rmask_a = row_mask(struct_first)
    rmask_b = row_mask(struct_second)
    cmask_a = col_mask(struct_first)
    cmask_b = col_mask(struct_second)
    part_a = product(panel_a, rmask_a)
    part_b = product(panel_b, rmask_b)
    row_a = -lax.psum(part_a, "prow") * cmask_a
    carried = jnp.einsum("av,cay->cvy", coupling, my_rows(row_a), precision=highest)
    row_b = -lax.psum(part_b + carried, "prow") * cmask_b
    chosen_a = matching(row_a)
    chosen_b = matching(row_b)
    mine_a = my_rows(row_a)
    mine_b = my_rows(row_b)
    term_a = jnp.einsum("rwy,rvy->wv", chosen_a, panel_a, precision=highest) * diagonal
    column_a = lax.psum(term_a, "prow")
    own_a = dinv_first - lax.psum(column_a, "pcol")
    own_rows = lax.dynamic_slice_in_dim(own_a, prow_index * slab, slab, 0)
    cross_term = (
        jnp.einsum("rvy,ray->va", panel_b * rmask_b, chosen_a, precision=highest)
        + jnp.einsum("av,aw->vw", coupling, own_rows, precision=highest)
    ) * diagonal
    own_term = jnp.einsum("rvy,ruy->vu", chosen_b, panel_b, precision=highest) * diagonal
    cross_col, own_col = lax.psum((cross_term, own_term), "prow")
    cross_sum, own_sum = lax.psum((cross_col, own_col), "pcol")
    cross = -cross_sum
    own_b = dinv_second - own_sum - jnp.dot(cross, coupling_full, precision=highest)
    out_a = mine_a.reshape(col_blocks, 1, slab, blk)
    out_b = mine_b.reshape(col_blocks, 1, slab, blk)
    return (out_a, own_a, out_b, cross, own_b)


def solution(mesh):
    return jax.shard_map(
        body,
        mesh=mesh,
        in_specs=(
            P(None, "prow", None, None, "pcol", None),
            P(None, "prow", "pcol", None),
            P(None, "prow", "pcol", None),
            P("prow", None),
            P(),
            P(),
            P(),
            P(),
        ),
        out_specs=(P(None, "pcol", "prow", None), P(), P(None, "pcol", "prow", None), P(), P()),
        check_vma=False,
    )
```

profile of v0, /device:TPU:1, one launch (start us, length us, event | category | flops | bytes accessed | tf_op | source)
XLA Modules:
  0.0 760.0 jit_solution(10065821596533365772)
XLA Ops:
  7.2 0.0 copy-start
  7.2 0.0 all-reduce.9.cloned.1.call-start
  7.2 0.8 convert_element_type.11
  8.0 0.1 reshape.44
  8.1 22.7 %all_gather.9 = f32[4,1,256,128]{3,2,0,1:T(8,128)S(1)} all-gather(f32[4,1,16,128]{3,2,0,1:T(8,128)} %bitcast.74), channel_id=1, replica_groups=mesh['prow'=32,'pcol'=16] {'pcol'}, dimensions={2}, use_global_device_ids=true | all-gather | bytes 557056 | tf_op jit(solution)/shard_map/all_gather | solution.py:49
  30.8 0.2 fusion.40
  31.0 0.0 copy-start.10
  31.0 0.0 copy-start.9
  31.0 3.1 fusion.4
  34.1 0.0 all-reduce.9.cloned.1.call-update
  34.1 0.0 all-reduce.15.cloned.1.call-start
  34.2 0.1 reshape.46
  34.3 0.1 reshape.49
  34.4 0.2 fusion.41
  34.6 0.2 dynamic-slice_reduce_fusion.1
  34.8 17.4 %all_gather.10 = f32[4,1,256,128]{3,2,0,1:T(8,128)S(1)} all-gather(f32[4,1,16,128]{3,2,0,1:T(8,128)S(1)} %bitcast.75), channel_id=1, replica_groups=mesh['prow'=32,'pcol'=16] {'pcol'}, dimensions={2}, use_global_device_ids=true | all-gather | bytes 557056 | tf_op jit(solution)/shard_map/all_gather | solution.py:50
  52.1 3.1 fusion.7
  55.3 134.7 %all-reduce.9.cloned.1.call-done = f32[8,256,128]{2,1,0:T(8,128)} async-done(((f32[8,256,128]{2,1,0:T(8,128)}), f32[8,256,128]{2,1,0:T(8,128)}) %all-reduce.9.cloned.1.call-update) | async-done | bytes 1048592 | tf_op jit(solution)/shard_map/psum | solution.py:58
  190.0 1.4 negate_multiply_fusion.1
  191.5 1.3 fusion.12
  192.8 2.0 fusion.10
  194.8 0.0 all-reduce.15.cloned.1.call-update
  194.8 0.0 all-reduce.11.cloned.1.call-start
  194.9 0.1 reshape.50
  195.0 0.2 dynamic-slice_reduce_fusion
  195.1 1.7 convolution_bitcast_fusion.2
  196.8 0.0 copy-start.6
  196.8 157.6 %all-reduce.15.cloned.1.call-done = (f32[256,256]{1,0:T(8,128)}, f32[8,256,128]{2,1,0:T(8,128)}) async-done(((f32[256,256]{1,0:T(8,128)}, f32[8,256,128]{2,1,0:T(8,128)}), (f32[256,256]{1,0:T(8,128)}, f32[8,256,128]{2,1,0:T(8,128)})) %all-reduce.15.cloned.1.call-update) | async-done | bytes 1310736 | tf_op jit(solution)/shard_map/psum | solution.py:66
  354.5 0.0 all-reduce.11.cloned.1.call-update
  354.5 0.0 all-reduce.13.cloned.1.call-start
  354.5 1.4 negate_multiply_fusion
  355.9 1.0 copy-done.3
  356.9 1.3 fusion.11
  358.2 113.8 %all-reduce.11.cloned.1.call-done = f32[256,256]{1,0:T(8,128)} async-done(((f32[256,256]{1,0:T(8,128)}), f32[256,256]{1,0:T(8,128)}) %all-reduce.11.cloned.1.call-update) | async-done | bytes 262160 | tf_op jit(solution)/shard_map/psum | solution.py:67
  472.1 1.0 sub.15
  473.1 0.0 copy-start.5
  473.1 1.1 fusion.14
  474.2 0.0 all-reduce.13.cloned.1.call-update
  474.2 0.0 all-reduce.17.cloned.1.call-start
  474.3 157.2 %all-reduce.13.cloned.1.call-done = (f32[256,256]{1,0:T(8,128)}, f32[256,256]{1,0:T(8,128)}) async-done(((f32[256,256]{1,0:T(8,128)}, f32[256,256]{1,0:T(8,128)}), (f32[256,256]{1,0:T(8,128)}, f32[256,256]{1,0:T(8,128)})) %all-reduce.13.cloned.1.call-update) | async-done | bytes 524304 | tf_op jit(solution)/shard_map/psum | solution.py:74
  631.5 0.0 all-reduce.17.cloned.1.call-update
  631.5 35.0 %all_gather.11 = f32[256,256]{1,0:T(8,128)S(1)} all-gather(f32[8,256]{1,0:T(8,128)S(1)} %copy-done.8), channel_id=1, replica_groups=mesh['prow'=32,'pcol'=16] {'prow'}, dimensions={0}, use_global_device_ids=true | all-gather | bytes 270336 | tf_op jit(solution)/shard_map/all_gather | solution.py:51
  666.6 1.4 dynamic-slice_bitcast_fusion.1
  668.0 1.4 dynamic-slice_bitcast_fusion
  669.3 81.0 %all-reduce.17.cloned.1.call-done = (f32[256,256]{1,0:T(8,128)}, f32[256,256]{1,0:T(8,128)}) async-done(((f32[256,256]{1,0:T(8,128)}, f32[256,256]{1,0:T(8,128)}), (f32[256,256]{1,0:T(8,128)}, f32[256,256]{1,0:T(8,128)})) %all-reduce.17.cloned.1.call-update) | async-done | bytes 524304 | tf_op jit(solution)/shard_map/psum | solution.py:75
  750.3 1.0 neg.11
  751.3 0.0 copy-start.4
  751.3 2.1 convolution_subtract_fusion
  (16 shorter events, 0.0 us)
Async XLA Ops:
  7.2 23.8 %copy-start = (f32[4,1,128,8,1,128]{5,4,3,2,1,0:T(1,128)S(1)}, f32[4,1,128,8,1,128]{5,4,3,2,1,0:T(1,128)}, u32[]{:S(2)}) copy-start(f32[4,1,128,8,1,128]{5,4,3,2,1,0:T(1,128)} %param.8) | copy-start | bytes 6291460
  7.2 182.8 %all-reduce.9.cloned.1.call-start = ((), (), s32[]{:S(2)}) async-start(), calls=%async_computation | async-start | bytes 2097152 | tf_op jit(solution)/shard_map/psum | solution.py:58
  31.0 3.3 copy-start.10
  31.0 3.8 copy-start.9
  34.1 320.3 %all-reduce.15.cloned.1.call-start = ((), (), s32[]{:S(2)}) async-start(), calls=%async_computation.3 | async-start | bytes 2621440 | tf_op jit(solution)/shard_map/psum | solution.py:66
  55.3 137.5 %copy-start.8 = (f32[8,256]{1,0:T(8,128)S(1)}, f32[8,256]{1,0:T(8,128)}, u32[]{:S(2)}) copy-start(f32[8,256]{1,0:T(8,128)} %param.11) | copy-start | bytes 24580
  190.0 2.8 copy-start.2
  191.4 1.3 copy-start.1
  194.8 277.2 %all-reduce.11.cloned.1.call-start = ((), (), s32[]{:S(2)}) async-start(), calls=%async_computation.1 | async-start | bytes 524288 | tf_op jit(solution)/shard_map/psum | solution.py:67
  196.8 275.3 %copy-start.6 = (f32[256,256]{1,0:T(8,128)S(1)}, f32[256,256]{1,0:T(8,128)}, u32[]{:S(2)}) copy-start(f32[256,256]{1,0:T(8,128)} %param.12) | copy-start | bytes 786436
  354.5 277.0 %all-reduce.13.cloned.1.call-start = ((), (), s32[]{:S(2)}) async-start(), calls=%async_computation.2 | async-start | bytes 1048576 | tf_op jit(solution)/shard_map/psum | solution.py:74
  355.9 1.0 copy-start.3
  358.2 393.1 %copy-start.7 = (f32[256,256]{1,0:T(8,128)S(1)}, f32[256,256]{1,0:T(8,128)}, u32[]{:S(2)}) copy-start(f32[256,256]{1,0:T(8,128)} %param.13) | copy-start | bytes 786436
  473.1 280.4 %copy-start.5 = (f32[256,256]{1,0:T(8,128)}, f32[256,256]{1,0:T(8,128)S(1)}, u32[]{:S(2)}) copy-start(f32[256,256]{1,0:T(8,128)S(1)} %sub.15) | copy-start | bytes 786436
  474.2 276.0 %all-reduce.17.cloned.1.call-start = ((), (), s32[]{:S(2)}) async-start(), calls=%async_computation.4 | async-start | bytes 1048576 | tf_op jit(solution)/shard_map/psum | solution.py:75
  751.3 2.2 copy-start.4
Sparse Core Ops, SparseCore 0:
  34.3 155.6 all-reduce.8
  195.0 159.4 all-reduce.14
  356.9 115.1 all-reduce.10
  475.9 155.5 all-reduce.12
  633.9 116.3 all-reduce.16
where the time goes:
time: 760 us
  waiting for transfers between devices  644 us (85%)
  blocking collectives  75.1 us (10%)
  matrix products  15.9 us (2%)
  between operations  13.9 us (2%)
    psum x1, waiting for transfers between devices, body(): column_a = lax.psum(term_a, 'prow')  158 us
    psum x1, waiting for transfers between devices, body(): cross_col, own_col = lax.psum((cross_term, own_term), 'prow')  157 us
    psum x1, waiting for transfers between devices, body(): row_a = -lax.psum(part_a, 'prow') * cmask_a  135 us
    psum x1, waiting for transfers between devices, body(): own_a = dinv_first - lax.psum(column_a, 'pcol')  114 us
    psum x1, waiting for transfers between devices, body(): cross_sum, own_sum = lax.psum((cross_col, own_col), 'pcol')  81 us
    all_gather x1, blocking collectives, body(): coupling_full = lax.all_gather(coupling, 'prow', axis=0, tiled=True)  35 us
    all_gather x1, blocking collectives, body(): panel_a = lax.all_gather(panel_first, 'pcol', axis=2, tiled=True)[:, 0]  22.7 us
    all_gather x1, blocking collectives, body(): panel_b = lax.all_gather(panel_second, 'pcol', axis=2, tiled=True)[:, 0]  17.4 us
  transfers between devices with their start and end apart: 5, of which 5 were waited for; matrix products, arithmetic and copies ran while one was open for 1% of the time, Pallas kernels for 0%

commit v1 on v0

v1 whole, which is shorter than its diff:
```python
import jax
import jax.numpy as jnp
from jax import lax
from jax.experimental import pallas as pl
from jax.experimental.pallas import tpu as pltpu
from jax.sharding import PartitionSpec as P

NX, NZ, NY = 4, 8, 8
F32, BF16 = jnp.float32, jnp.bfloat16
MESH = pl.DeviceIdType.MESH

NN = (((1,), (0,)), ((), ()))
NT = (((1,), (1,)), ((), ()))


def split(v):
    hi = v.astype(BF16)
    return hi, (v - hi.astype(F32)).astype(BF16)


def dot3(a, b, dims=NN):
    def one(u, v):
        return lax.dot_general(u, v, dims, preferred_element_type=F32)

    return one(a[0], b[0]) + (one(a[0], b[1]) + one(a[1], b[0]))


def steps_of(way, half):
    return 4 if (way == 0) == (half == 0) else 3


def kernel(
    g_hbm, a_hbm, b_hbm, c_hbm, d1_hbm, d2_hbm, s1, s2,
    out_a, own_1, out_b, cross_out, own_2,
    g_raw, g_hi, g_lo, full, p_hi, p_lo, c_full, d1, d2,
    pa, pb, za, sb,
    xa_mid, xa_fin, xb_mid, xb_fin, za_in, zb_in,
    se, ex, pt, rr, tile, fin,
    load_sem, own_sem,
    ag_send, ag_recv, sib_send, sib_recv, c_send, c_recv,
    xa_send, xa_recv, xb_send, xb_recv, za_send, za_recv, zb_send, zb_recv,
    ex_send, ex_recv, rr_send, rr_recv, yz_send, yz_recv,
    fx_send, fx_recv, fs_send, fs_recv,
):
    p = lax.axis_index("prow")
    q = lax.axis_index("pcol")
    x, z = p // NZ, lax.rem(p, NZ)
    y, core = q // 2, lax.rem(q, 2)

    def at_x(k):
        return lax.rem(x + k, NX)

    def at_z(k):
        return lax.rem(z + k, NZ)

    def at_y(k):
        return lax.rem(y + k, NY)

    sibling = (p, y * 2 + 1 - core)

    def remote(src, dst, send, recv, where):
        return pltpu.make_async_remote_copy(
            src_ref=src, dst_ref=dst, send_sem=send, recv_sem=recv,
            device_id=where, device_id_type=MESH,
        )

    loads = [
        pltpu.make_async_copy(g_hbm, g_raw, load_sem.at[0]),
        pltpu.make_async_copy(d1_hbm, d1, load_sem.at[1]),
        pltpu.make_async_copy(d2_hbm, d2, load_sem.at[2]),
    ]
    rows16 = pl.ds(pl.multiple_of(q * 16, 16), 16)
    rows8 = pl.ds(pl.multiple_of(p * 8, 8), 8)
    own = [
        pltpu.make_async_copy(a_hbm, full.at[0, :, rows16], own_sem.at[0]),
        pltpu.make_async_copy(b_hbm, full.at[1, :, rows16], own_sem.at[1]),
        pltpu.make_async_copy(c_hbm, c_full.at[rows8], own_sem.at[2]),
    ]
    for copy in own + loads:
        copy.start()

    barrier = pltpu.get_barrier_semaphore()
    for where in ((p, at_y(1) * 2 + core), (p, at_y(NY - 1) * 2 + core), sibling):
        pl.semaphore_signal(barrier, inc=1, device_id=where, device_id_type=MESH)

    def greet(k, carry):
        pl.semaphore_signal(
            barrier, inc=1, device_id=(lax.rem(p + k, NX * NZ), q), device_id_type=MESH
        )
        return carry

    lax.fori_loop(1, NX * NZ, greet, 0)
    pl.semaphore_wait(barrier, NX * NZ - 1 + 3)

    for copy in own:
        copy.wait()

    ends = []

    def shard(k, rows):
        return full.at[k, :, pl.ds(pl.multiple_of(rows * 16, 16), 16)]

    def hops(k, way):
        return 4 if k == way else 3

    def ring_send(k, way, step):
        back = step - 1
        from_y = at_y(NY - back) if way == 0 else at_y(back)
        to_y = at_y(1) if way == 0 else at_y(NY - 1)
        ref = shard(k, from_y * 2 + core)
        copy = remote(
            ref, ref, ag_send.at[k, way, step - 1], ag_recv.at[k, way, step - 1],
            (p, to_y * 2 + core),
        )
        copy.start()
        ends.append(copy)
        return copy

    def across(k, index, row_y):
        ref = shard(k, row_y * 2 + core)
        copy = remote(ref, ref, sib_send.at[k, index], sib_recv.at[k, index], sibling)
        copy.start()
        ends.append(copy)
        return copy

    pending = {}
    crossing = {0: [], 1: []}
    for k in (0, 1):
        for way in (0, 1):
            pending[k, way] = ring_send(k, way, 1)
    for k in (0, 1):
        crossing[k].append(across(k, 0, y))

    def c_start(k, carry):
        remote(
            c_full.at[rows8], c_full.at[rows8], c_send.at[k], c_recv.at[k],
            (lax.rem(p + k, NX * NZ), q),
        ).start()
        return carry

    lax.fori_loop(1, NX * NZ, c_start, 0)

    loads[0].wait()

    def split_g(c, carry):
        hi, lo = split(g_raw[pl.ds(c, 512, stride=8), :])
        columns = pl.ds(pl.multiple_of(c * 128, 128), 128)
        g_hi[:, columns] = hi
        g_lo[:, columns] = lo
        return carry

    lax.fori_loop(0, 8, split_g, 0)

    for step in range(1, 5):
        for k in (0, 1):
            for way in (0, 1):
                if step > hops(k, way):
                    continue
                pending[k, way].wait_recv()
                if step < hops(k, way):
                    pending[k, way] = ring_send(k, way, step + 1)
                row_y = at_y(NY - step) if way == 0 else at_y(step)
                crossing[k].append(across(k, len(crossing[k]), row_y))

    def prepare(k, struct):
        for copy in crossing[k]:
            copy.wait_recv()
        for r in range(4):
            mask = struct[r * (NX * NZ) + p].astype(F32)
            hi, lo = split(full[k, r] * mask)
            p_hi[k, :, r * 128:(r + 1) * 128] = hi
            p_lo[k, :, r * 128:(r + 1) * 128] = lo

    def col_mask(struct, c):
        return struct[c * (NY * 2) + q].astype(F32)

    prepare(0, s1)

    def mul_a(t, carry):
        columns = pl.ds(pl.multiple_of(t * 256, 256), 256)
        r = dot3((p_hi[0], p_lo[0]), (g_hi[:, columns], g_lo[:, columns]))
        pa[:, :, :, columns] = r.reshape(NX, NZ, 8, 256)
        return carry

    lax.fori_loop(0, 4, mul_a, 0)

    def x_start(piece, mid, last, send, recv):
        right, left = (at_x(1) * NZ + z, q), (at_x(NX - 1) * NZ + z, q)
        copies = {
            "far0": remote(piece(at_x(2), 0), mid.at[0], send.at[0], recv.at[0], right),
            "far1": remote(piece(at_x(2), 1), mid.at[1], send.at[1], recv.at[1], left),
            "near1": remote(piece(at_x(1), 1), last.at[0, 1], send.at[2], recv.at[2], right),
            "near0": remote(piece(at_x(3), 0), last.at[1, 0], send.at[3], recv.at[3], left),
            "sum0": remote(piece(at_x(1), 0), last.at[0, 0], send.at[4], recv.at[4], right),
            "sum1": remote(piece(at_x(3), 1), last.at[1, 1], send.at[5], recv.at[5], left),
        }
        for name in ("far0", "far1", "near1", "near0"):
            copies[name].start()
        ends.extend(copies.values())
        return copies

    def x_middle(copies, add, mid):
        copies["far0"].wait_recv()
        add(at_x(1), 0, mid)
        copies["sum0"].start()
        copies["far1"].wait_recv()
        add(at_x(3), 1, mid)
        copies["sum1"].start()

    def x_wait(copies):
        for name in ("near1", "near0", "sum0", "sum1"):
            copies[name].wait_recv()

    def xa_piece(d, half):
        return pa.at[d, half * 4:(half + 1) * 4]

    def xa_add(d, half, mid):
        pa[d, half * 4:(half + 1) * 4] += mid[half]

    xa = x_start(xa_piece, xa_mid, xa_fin, xa_send, xa_recv)

    def c_wait(k, carry):
        remote(
            c_full.at[rows8], c_full.at[rows8], c_send.at[k], c_recv.at[k],
            (lax.rem(p + k, NX * NZ), q),
        ).wait()
        return carry

    lax.fori_loop(1, NX * NZ, c_wait, 0)
    coupling = c_full[...]
    c_parts = split(coupling)
    ct_parts = split(coupling.T)

    prepare(1, s2)

    def mul_b(t, carry):
        columns = pl.ds(pl.multiple_of(t * 256, 256), 256)
        r = dot3((p_hi[1], p_lo[1]), (g_hi[:, columns], g_lo[:, columns]))
        first = pa[:, :, :, columns].reshape(256, 256)
        lane = lax.broadcasted_iota(jnp.int32, (256, 256), 1)
        masks = jnp.where(lane < 128, col_mask(s1, 2 * t), col_mask(s1, 2 * t + 1))
        r = r - dot3(ct_parts, split(first * masks))
        pb[:, :, :, columns] = r.reshape(NX, NZ, 8, 256)
        return carry

    lax.fori_loop(0, 4, mul_b, 0)

    def z_copy(piece, into, send, recv, way, half, step):
        n = steps_of(way, half)
        away = n - step + 1
        d = at_z(away) if way == 0 else at_z(NZ - away)
        to_z = at_z(1) if way == 0 else at_z(NZ - 1)
        return remote(
            piece(d, half), into.at[way, half, step - 1],
            send.at[way, half, step - 1], recv.at[way, half, step - 1],
            (x * NZ + to_z, q),
        )

    def z_step(piece, add, into, send, recv, step):
        for half in (0, 1):
            for way in (0, 1):
                n = steps_of(way, half)
                if step > n:
                    continue
                copy = z_copy(piece, into, send, recv, way, half, step)
                if step > 1:
                    z_copy(piece, into, send, recv, way, half, step - 1).wait_recv()
                    away = n - step + 1
                    d = at_z(away) if way == 0 else at_z(NZ - away)
                    add(d, half, into.at[way, half, step - 2])
                copy.start()
                ends.append(copy)

    def z_wait(piece, into, send, recv):
        for half in (0, 1):
            for way in (0, 1):
                z_copy(piece, into, send, recv, way, half, steps_of(way, half)).wait_recv()

    def zb_piece(d, half):
        return pb.at[half * 2:(half + 1) * 2, d]

    def zb_add(d, half, ref):
        pb[half * 2:(half + 1) * 2, d] += ref[...]

    def za_piece(d, half):
        return za.at[d, :, half * 512:(half + 1) * 512]

    def za_add(d, half, ref):
        za[d, :, half * 512:(half + 1) * 512] += ref[...]

    zb = (zb_piece, zb_add, zb_in, zb_send, zb_recv)
    zz = (za_piece, za_add, za_in, za_send, za_recv)

    z_step(*zb, 1)
    x_middle(xa, xa_add, xa_mid)
    z_step(*zb, 2)
    z_step(*zb, 3)
    x_wait(xa)
    for half in (0, 1):
        rows = slice(half * 4, half * 4 + 4)
        za[rows] = pa[x, rows] + xa_fin[0, half] + xa_fin[1, half]
    z_step(*zz, 1)
    z_step(*zb, 4)
    z_step(*zz, 2)

    z_wait(zb_piece, zb_in, zb_send, zb_recv)
    for half in (0, 1):
        rows = slice(half * 2, half * 2 + 2)
        sb[rows] = (
            pb[rows, z]
            + zb_in[0, half, steps_of(0, half) - 1]
            + zb_in[1, half, steps_of(1, half) - 1]
        )

    def xb_piece(d, half):
        return sb.at[d, :, half * 512:(half + 1) * 512]

    def xb_add(d, half, mid):
        sb[d, :, half * 512:(half + 1) * 512] += mid[half]

    xb = x_start(xb_piece, xb_mid, xb_fin, xb_send, xb_recv)
    z_step(*zz, 3)
    x_middle(xb, xb_add, xb_mid)
    z_step(*zz, 4)

    def deliver(which, half, value, struct, out):
        for k in range(4):
            c = half * 4 + k
            block = value[:, k * 128:(k + 1) * 128] * (-col_mask(struct, c))
            out[c] = block
            r = c // 2
            se[c % 2, which, :, r * 128:(r + 1) * 128] = block

    to_col = 2 * z + 1 - lax.rem(x, 2)
    slot = x // 2

    def hand_over(which):
        for parity in (0, 1):
            copy = remote(
                se.at[parity, which], ex.at[slot, which],
                ex_send.at[parity, which], ex_recv.at[slot, which],
                (q + 16 * parity, to_col),
            )
            copy.start()
            ends.append(copy)

    def taken(which):
        for s in (0, 1):
            remote(
                se.at[0, which], ex.at[s, which], ex_send.at[0, which], ex_recv.at[s, which],
                sibling,
            ).wait_recv()

    z_wait(za_piece, za_in, za_send, za_recv)
    for half in (0, 1):
        value = (
            za[z, :, half * 512:(half + 1) * 512]
            + za_in[0, half, steps_of(0, half) - 1]
            + za_in[1, half, steps_of(1, half) - 1]
        )
        deliver(0, half, value, s1, out_a)
    hand_over(0)
    x_wait(xb)
    for half in (0, 1):
        value = sb[x, :, half * 512:(half + 1) * 512] + xb_fin[0, half] + xb_fin[1, half]
        deliver(1, half, value, s2, out_b)
    hand_over(1)

    taken(0)
    ra = split(ex[:, 0].reshape(16, 512))
    parts = [
        dot3(ra, (p_hi[0], p_lo[0]), NT),
        dot3(ra, (p_hi[1], p_lo[1]), NT),
    ]
    taken(1)
    rb = split(ex[:, 1].reshape(16, 512))
    parts.append(dot3(rb, (p_hi[1], p_lo[1]), NT))
    for m in range(3):
        for s in range(2):
            for h in range(2):
                pt[m, s * 2 + h] = parts[m][s * 8:(s + 1) * 8, h * 128:(h + 1) * 128]

    def at_sum(m, j):
        return j * NZ + lax.rem(y + 3 * m, NZ)

    def tile_copy(m, j):
        return remote(
            pt.at[m, j], rr.at[p], rr_send.at[m, j], rr_recv.at[p], (at_sum(m, j), q)
        )

    for m in range(3):
        for j in range(4):
            @pl.when(at_sum(m, j) != p)
            def _():
                tile_copy(m, j).start()

    turn = lax.rem(z - y + NZ, NZ)
    mine = turn // 3
    sums = lax.rem(turn, 3) == 0
    block = fin.at[core, x]

    @pl.when(sums)
    def _():
        rr[p] = pt[mine, x]

        def arrived(k, carry):
            src = lax.rem(p + k, NX * NZ)
            remote(
                pt.at[0, 0], rr.at[src], rr_send.at[0, 0], rr_recv.at[src], sibling
            ).wait_recv()
            return carry

        lax.fori_loop(1, NX * NZ, arrived, 0)
        tile[...] = jnp.sum(rr[...], axis=0)
        place = fin.at[core, x, mine, y]
        local = pltpu.make_async_copy(tile, place, yz_recv.at[0])
        local.start()

        def spread(k, carry):
            remote(
                tile, place, yz_send.at[k], yz_recv.at[0],
                (x * NZ + lax.rem(z + k // NY, NZ), lax.rem(y + lax.rem(k, NY), NY) * 2 + core),
            ).start()
            return carry

        lax.fori_loop(1, NY * NZ, spread, 0)

    pltpu.make_async_copy(block, block, yz_recv.at[0]).wait()

    right, left = (at_x(1) * NZ + z, q), (at_x(NX - 1) * NZ + z, q)

    def block_to(origin, where, index):
        ref = fin.at[core, origin]
        return remote(ref, ref, fx_send.at[index], fx_recv.at[index], where)

    def half_to(origin, half, where, index):
        ref = fin.at[core, origin, :, half * 4:(half + 1) * 4]
        return remote(ref, ref, fx_send.at[index], fx_recv.at[index], where)

    def block_across(origin, index):
        ref = fin.at[core, origin]
        copy = remote(ref, ref, fs_send.at[index], fs_recv.at[index], sibling)
        copy.start()
        ends.append(copy)
        return copy

    to_right, to_left = block_to(x, right, 0), block_to(x, left, 1)
    to_right.start()
    to_left.start()
    over = [block_across(x, 0)]
    to_right.wait_recv()
    on_right = half_to(at_x(3), 0, right, 2)
    on_right.start()
    over.append(block_across(at_x(3), 1))
    to_left.wait_recv()
    on_left = half_to(at_x(1), 1, left, 3)
    on_left.start()
    over.append(block_across(at_x(1), 2))
    on_right.wait_recv()
    on_left.wait_recv()
    over.append(block_across(at_x(2), 3))
    ends.extend((to_right, to_left, on_right, on_left))
    for copy in over:
        copy.wait_recv()

    loads[1].wait()
    loads[2].wait()
    cross_t = []
    for co in range(2):
        for xo in range(4):
            xs, h = (1 - co) + 2 * (xo // 2), xo % 2
            rows, columns = slice(xs * 64, xs * 64 + 64), slice(h * 128, h * 128 + 128)
            own_1[rows, columns] = d1[rows, columns] - fin[co, xo, 0].reshape(64, 128)
            cross_out[rows, columns] = fin[co, xo, 1].reshape(64, 128)
            d2[rows, columns] = d2[rows, columns] - fin[co, xo, 2].reshape(64, 128)
    cross = -(cross_out[...].T + dot3(ct_parts, split(own_1[...])))
    cross_out[...] = cross
    own_2[...] = d2[...] - dot3(split(cross), c_parts)

    for copy in ends:
        copy.wait_send()
    for m in range(3):
        for j in range(4):
            @pl.when(at_sum(m, j) != p)
            def _():
                tile_copy(m, j).wait_send()

    @pl.when(sums)
    def _():
        def spread_end(k, carry):
            remote(tile, tile, yz_send.at[k], yz_recv.at[0], sibling).wait_send()
            return carry

        lax.fori_loop(1, NY * NZ, spread_end, 0)


def body(
    inverse_block,
    panel_first,
    panel_second,
    coupling,
    dinv_first,
    dinv_second,
    struct_first,
    struct_second,
):
    dma = pltpu.SemaphoreType.DMA
    any_space = pl.BlockSpec(memory_space=pl.ANY)
    smem = pl.BlockSpec(memory_space=pltpu.SMEM)
    vmem = pl.BlockSpec(memory_space=pltpu.VMEM)
    square = jax.ShapeDtypeStruct((256, 256), F32)
    rows = jax.ShapeDtypeStruct((8, 8, 128), F32)
    row_a, own_a, row_b, cross, own_b = pl.pallas_call(
        kernel,
        out_shape=(rows, square, rows, square, square),
        in_specs=[any_space] * 6 + [smem] * 2,
        out_specs=(vmem,) * 5,
        scratch_shapes=[
            pltpu.VMEM((4096, 128), F32),
            pltpu.VMEM((512, 1024), BF16),
            pltpu.VMEM((512, 1024), BF16),
            pltpu.VMEM((2, 4, 256, 128), F32),
            pltpu.VMEM((2, 256, 512), BF16),
            pltpu.VMEM((2, 256, 512), BF16),
            pltpu.VMEM((256, 256), F32),
            pltpu.VMEM((256, 256), F32),
            pltpu.VMEM((256, 256), F32),
            pltpu.VMEM((4, 8, 8, 1024), F32),
            pltpu.VMEM((4, 8, 8, 1024), F32),
            pltpu.VMEM((8, 8, 1024), F32),
            pltpu.VMEM((4, 8, 1024), F32),
            pltpu.VMEM((2, 4, 8, 1024), F32),
            pltpu.VMEM((2, 2, 4, 8, 1024), F32),
            pltpu.VMEM((2, 8, 512), F32),
            pltpu.VMEM((2, 2, 8, 512), F32),
            pltpu.VMEM((2, 2, 4, 8, 512), F32),
            pltpu.VMEM((2, 2, 4, 2, 8, 1024), F32),
            pltpu.VMEM((2, 2, 8, 512), F32),
            pltpu.VMEM((2, 2, 8, 512), F32),
            pltpu.VMEM((3, 4, 8, 128), F32),
            pltpu.VMEM((32, 8, 128), F32),
            pltpu.VMEM((8, 128), F32),
            pltpu.VMEM((2, 4, 3, 8, 8, 128), F32),
            dma((3,)), dma((3,)),
            dma((2, 2, 4)), dma((2, 2, 4)), dma((2, 8)), dma((2, 8)), dma((32,)), dma((32,)),
            dma((6,)), dma((6,)), dma((6,)), dma((6,)),
            dma((2, 2, 4)), dma((2, 2, 4)), dma((2, 2, 4)), dma((2, 2, 4)),
            dma((2, 2)), dma((2, 2)), dma((3, 4)), dma((32,)), dma((64,)), dma((1,)),
            dma((4,)), dma((4,)), dma((4,)), dma((4,)),
        ],
        compiler_params=pltpu.CompilerParams(
            collective_id=0, has_side_effects=True, vmem_limit_bytes=40 * 1024 * 1024
        ),
        name="selected_inversion",
    )(
        inverse_block.reshape(4096, 128),
        panel_first.reshape(4, 16, 128),
        panel_second.reshape(4, 16, 128),
        coupling, dinv_first, dinv_second, struct_first, struct_second,
    )
    return (
        row_a.reshape(8, 1, 8, 128), own_a, row_b.reshape(8, 1, 8, 128), cross, own_b,
    )


def solution(mesh):
    return jax.shard_map(
        body,
        mesh=mesh,
        in_specs=(
            P(None, "prow", None, None, "pcol", None),
            P(None, "prow", "pcol", None),
            P(None, "prow", "pcol", None),
            P("prow", None),
            P(),
            P(),
            P(),
            P(),
        ),
        out_specs=(P(None, "pcol", "prow", None), P(), P(None, "pcol", "prow", None), P(), P()),
        check_vma=False,
    )
```

time: 760 us -> 107 us (0.14)
  waiting for transfers between devices: 644 us -> 0 us
  Pallas kernels: 0 us -> 95.3 us
  blocking collectives: 75.1 us -> 0 us
  matrix products: 15.9 us -> 0 us
  between operations: 13.9 us -> 0.66 us
    psum x5 -> x0, waiting for transfers between devices: 644 us -> none  [the longest x1 158 us: body(): column_a = lax.psum(term_a, 'prow')]
    pallas_call x0 -> x1, Pallas kernels: none -> 95.3 us  [body(): pl.pallas_call(kernel, out_shape=(rows, square, rows, square, square), in...]
    all_gather x3 -> x0, blocking collectives: 75.1 us -> none  [the longest x1 35 us: body(): coupling_full = lax.all_gather(coupling, 'prow', axis=0, tiled=True)]
    dot_general x8 -> x0, matrix products: 15.9 us -> none  [the longest x2 6.26 us: product(): return jnp.einsum('rwx,rxcy->cwy', panel * mask, local, precision=highest)]
    unnamed x22 -> x21, local copies, waits for them, and re-layouts: 1.07 us -> 10.3 us
  transfers between devices with their start and end apart: 5 -> 0, of which waited for: 5 -> 0; matrix products, arithmetic and copies ran while one was open for 1% -> 0% of each run, Pallas kernels for 0% -> 0%
where the time goes in v1:
time: 107 us; the launch traced here: 106 us
  Pallas kernels  95.3 us (89%)
  local copies, waits for them, and re-layouts  10.3 us (10%)
    pallas_call x1, Pallas kernels, body(): pl.pallas_call(kernel, out_shape=(rows, square, rows, square, square), in...  95.3 us
    unnamed x21, local copies, waits for them, and re-layouts  10.3 us

profile of v1, /device:TPU:1, one launch (start us, length us, event | category | flops | bytes accessed | tf_op | source)
XLA Modules:
  0.0 106.3 jit_solution(15450135530900547647)
XLA Ops:
  0.6 0.0 copy-start
  0.6 1.6 %copy-done = f32[4,1,128,8,1,128]{5,4,3,2,1,0:T(1,128)S(1)} copy-done((f32[4,1,128,8,1,128]{5,4,3,2,1,0:T(1,128)S(1)}, f32[4,1,128,8,1,128]{5,4,3,2,1,0:T(1,128)}, u32[]{:S(2)}) %copy-start) | copy-done | bytes 2097176
  2.2 0.0 copy-start.1
  2.2 0.9 copy-done.1
  3.2 0.0 copy-start.2
  3.2 0.9 copy-done.2
  4.1 0.0 copy-start.3
  4.1 0.8 copy-done.3
  4.9 0.0 copy-start.4
  4.9 0.8 copy-done.4
  5.6 0.0 copy-start.5
  5.6 0.7 copy-done.5
  6.3 0.0 copy-start.6
  6.3 0.7 copy-done.6
  7.0 0.0 copy-start.7
  7.0 0.7 copy-done.7
  7.7 95.3 %selected_inversion.1 = (f32[8,8,128]{2,1,0:T(8,128)S(1)}, f32[256,256]{1,0:T(8,128)S(1)}, f32[8,8,128]{2,1,0:T(8,128)S(1)}, f32[256,256]{1,0:T(8,128)S(1)}, f32[256,256]{1,0:T(8,128)S(1)}) custom-call(f32[4096,128]{1,0:T(8,128)S(1)} %bitcast.9, f32[4,16,128]{2,1,0:T(8,128)S(1)} %bitcast.10, f32[4,16,128]{2,1,0:T(8,128)S(1)} %bitcast.11, ...), custom_call_target="tpu_custom_call" | custom-call | tf_op jit(solution)/shard_map/selected_inversion/pallas_call | solution.py:513
  102.9 0.6 copy.20
  103.5 0.7 copy.21
  104.2 0.6 copy.22
  104.8 0.7 copy.23
  105.6 0.7 copy.24
Async XLA Ops:
  0.6 1.6 %copy-start = (f32[4,1,128,8,1,128]{5,4,3,2,1,0:T(1,128)S(1)}, f32[4,1,128,8,1,128]{5,4,3,2,1,0:T(1,128)}, u32[]{:S(2)}) copy-start(f32[4,1,128,8,1,128]{5,4,3,2,1,0:T(1,128)} %param.8) | copy-start | bytes 6291460
  2.2 0.9 copy-start.1
  3.2 0.9 copy-start.2
  4.1 0.8 copy-start.3
  4.9 0.8 copy-start.4
  5.6 0.7 copy-start.5
  6.3 0.7 copy-start.6
  7.0 0.7 copy-start.7

commit v2 on v0

v2 whole, which is shorter than its diff:
```python
import jax
import jax.numpy as jnp
from jax import lax
from jax.experimental import pallas as pl
from jax.experimental.pallas import tpu as pltpu
from jax.sharding import PartitionSpec as P

NX, NZ, NY = 4, 8, 8
F32, BF16 = jnp.float32, jnp.bfloat16
MESH = pl.DeviceIdType.MESH

NN = (((1,), (0,)), ((), ()))
NT = (((1,), (1,)), ((), ()))


def split(v):
    hi = v.astype(BF16)
    return hi, (v - hi.astype(F32)).astype(BF16)


def dot3(a, b, dims=NN):
    def one(u, v):
        return lax.dot_general(u, v, dims, preferred_element_type=F32)

    return one(a[0], b[0]) + (one(a[0], b[1]) + one(a[1], b[0]))


def steps_of(way, half):
    return 4 if (way == 0) == (half == 0) else 3


def kernel(
    g_hbm, a_hbm, b_hbm, c_hbm, d1_hbm, d2_hbm, s1_hbm, s2_hbm,
    out_a, own_1, out_b, cross_out, own_2,
    s1, s2, g_raw, g_hi, g_lo, full, p_hi, p_lo, c_full, d1, d2,
    pa, pb, za, sb,
    xa_mid, xa_fin, xb_in, za_in, zb_in,
    rows_1, rows_2, ex_a, ex_b, pt, rr, tile, fin, all_sent,
    load_sem, own_sem,
    ag_send, ag_recv, sib_send, sib_recv, cz_send, cz_recv, cx_send, cx_recv,
    xa_send, xa_recv, xb_send, xb_recv, za_send, za_recv, zb_send, zb_recv,
    exa_send, exa_recv, exb_send, exb_recv, rr_send, rr_recv, yz_send, yz_recv,
    fx_send, fx_recv, fs_send, fs_recv,
):
    p = lax.axis_index("prow")
    q = lax.axis_index("pcol")
    x, z = p // NZ, lax.rem(p, NZ)
    y, core = q // 2, lax.rem(q, 2)

    def at_x(k):
        return lax.rem(x + k + NX, NX)

    def at_z(k):
        return lax.rem(z + k + NZ, NZ)

    def at_y(k):
        return lax.rem(y + k + NY, NY)

    sibling = (p, y * 2 + 1 - core)

    def remote(src, dst, send, recv, where):
        return pltpu.make_async_remote_copy(
            src_ref=src, dst_ref=dst, send_sem=send, recv_sem=recv,
            device_id=where, device_id_type=MESH,
        )

    rows16 = pl.ds(pl.multiple_of(q * 16, 16), 16)
    rows8 = pl.ds(pl.multiple_of(p * 8, 8), 8)
    own = [
        pltpu.make_async_copy(a_hbm, full.at[0, :, rows16], own_sem.at[0]),
        pltpu.make_async_copy(b_hbm, full.at[1, :, rows16], own_sem.at[1]),
        pltpu.make_async_copy(c_hbm, c_full.at[rows8], own_sem.at[2]),
    ]
    loads = [
        pltpu.make_async_copy(g_hbm, g_raw, load_sem.at[0]),
        pltpu.make_async_copy(d1_hbm, d1, load_sem.at[1]),
        pltpu.make_async_copy(d2_hbm, d2, load_sem.at[2]),
        pltpu.make_async_copy(s1_hbm, s1, load_sem.at[3]),
        pltpu.make_async_copy(s2_hbm, s2, load_sem.at[4]),
    ]
    for copy in own + loads:
        copy.start()

    barrier = pltpu.get_barrier_semaphore()
    near = [(p, at_y(k) * 2 + core) for k in (1, -1, 2, -2)] + [sibling]
    near += [(x * NZ + at_z(k), q) for k in range(1, NZ)]
    near += [(at_x(k) * NZ + z, q) for k in range(1, NX)]
    for where in near:
        pl.semaphore_signal(barrier, inc=1, device_id=where, device_id_type=MESH)
    pl.semaphore_wait(barrier, len(near))

    for copy in own:
        copy.wait()

    ends = []

    def shard(k, row_y):
        rows = row_y * 2 + core
        return full.at[k, :, pl.ds(pl.multiple_of(rows * 16, 16), 16)]

    def ring(k, of, to):
        ref = shard(k, at_y(of))
        return remote(
            ref, ref, ag_send.at[k, of - to + 4], ag_recv.at[k, of - to + 4],
            (p, at_y(to) * 2 + core),
        )

    def push(k, of, to):
        copy = ring(k, of, to)
        copy.start()
        ends.append(copy)

    crossing = {0: [], 1: []}

    def across(k, of):
        ref = shard(k, at_y(of))
        copy = remote(ref, ref, sib_send.at[k, of + 4], sib_recv.at[k, of + 4], sibling)
        copy.start()
        ends.append(copy)
        crossing[k].append(copy)

    def got(k, of):
        ring(k, of, 0).wait_recv()
        across(k, of)

    for k in (0, 1):
        for to in (2, -2, 1, -1):
            push(k, 0, to)
        across(k, 0)

    def cz_copy(k):
        return remote(
            c_full.at[rows8], c_full.at[rows8], cz_send.at[k], cz_recv.at[k],
            (x * NZ + at_z(k), q),
        )

    for k in range(1, NZ):
        cz_copy(k).start()

    for index in (0, 3, 4):
        loads[index].wait()

    def split_g(c, carry):
        hi, lo = split(g_raw[pl.ds(c, 512, stride=8), :])
        columns = pl.ds(pl.multiple_of(c * 128, 128), 128)
        g_hi[:, columns] = hi
        g_lo[:, columns] = lo
        return carry

    lax.fori_loop(0, 8, split_g, 0)

    for k in (0, 1):
        for of in (-2, 2):
            got(k, of)
            way = 1 if of < 0 else -1
            push(k, of, way)
            if (of < 0) == (k == 0):
                push(k, of, 2 * way)
        got(k, -1)
        got(k, 1)

    for k in range(1, NZ):
        cz_copy(k).wait_recv()
    rows64 = pl.ds(pl.multiple_of(x * 64, 64), 64)

    def cx_copy(k):
        return remote(
            c_full.at[rows64], c_full.at[rows64], cx_send.at[k], cx_recv.at[k],
            (at_x(k) * NZ + z, q),
        )

    for k in range(1, NX):
        cx_copy(k).start()

    def prepare(k, struct):
        for of in (-3, 3, -4 if k == 0 else 4):
            got(k, of)
        for copy in crossing[k]:
            copy.wait_recv()
        for r in range(4):
            mask = struct[r * (NX * NZ) + p].astype(F32)
            hi, lo = split(full[k, r] * mask)
            p_hi[k, :, r * 128:(r + 1) * 128] = hi
            p_lo[k, :, r * 128:(r + 1) * 128] = lo

    def col_mask(struct, c):
        return struct[c * (NY * 2) + q].astype(F32)

    prepare(0, s1)

    def mul_a(t, carry):
        columns = pl.ds(pl.multiple_of(t * 256, 256), 256)
        r = dot3((p_hi[0], p_lo[0]), (g_hi[:, columns], g_lo[:, columns]))
        pa[:, :, t, 0] = r[:, :128].reshape(NX, NZ, 8, 128)
        pa[:, :, t, 1] = r[:, 128:].reshape(NX, NZ, 8, 128)
        return carry

    lax.fori_loop(0, 4, mul_a, 0)

    x_right, x_left = (at_x(1) * NZ + z, q), (at_x(-1) * NZ + z, q)

    def xa_piece(d, half):
        return pa.at[d, half * 4:(half + 1) * 4]

    def xa_copy(index, d, half, into, where):
        return remote(xa_piece(d, half), into, xa_send.at[index], xa_recv.at[index], where)

    xa = {
        "far0": xa_copy(0, at_x(2), 0, xa_mid.at[0], x_right),
        "far1": xa_copy(1, at_x(2), 1, xa_mid.at[1], x_left),
        "near1": xa_copy(2, at_x(1), 1, xa_fin.at[0, 1], x_right),
        "near0": xa_copy(3, at_x(3), 0, xa_fin.at[1, 0], x_left),
        "sum0": xa_copy(4, at_x(1), 0, xa_fin.at[0, 0], x_right),
        "sum1": xa_copy(5, at_x(3), 1, xa_fin.at[1, 1], x_left),
    }
    for name in ("far0", "far1", "near1", "near0"):
        xa[name].start()
    ends.extend(xa.values())

    for k in range(1, NX):
        cx_copy(k).wait_recv()
    coupling = c_full[...]
    c_parts = split(coupling)
    ct_parts = split(coupling.T)

    prepare(1, s2)

    def mul_b(t, carry):
        columns = pl.ds(pl.multiple_of(t * 256, 256), 256)
        r = dot3((p_hi[1], p_lo[1]), (g_hi[:, columns], g_lo[:, columns]))
        first = jnp.concatenate(
            [pa[:, :, t, h].reshape(256, 128) * col_mask(s1, 2 * t + h) for h in (0, 1)], axis=1
        )
        r = r - dot3(ct_parts, split(first))
        pb[:, :, t, 0] = r[:, :128].reshape(NX, NZ, 8, 128)
        pb[:, :, t, 1] = r[:, 128:].reshape(NX, NZ, 8, 128)
        return carry

    lax.fori_loop(0, 4, mul_b, 0)

    def zb_copy(way, half, step):
        away = steps_of(way, half) - step + 1
        d = at_z(away) if way == 0 else at_z(-away)
        to_z = at_z(1) if way == 0 else at_z(-1)
        return d, remote(
            pb.at[half * 2:(half + 1) * 2, d], zb_in.at[way, half, step - 1],
            zb_send.at[way, half, step - 1], zb_recv.at[way, half, step - 1],
            (x * NZ + to_z, q),
        )

    def zb_step(step):
        for half in (0, 1):
            for way in (0, 1):
                if step > steps_of(way, half):
                    continue
                d, copy = zb_copy(way, half, step)
                if step > 1:
                    zb_copy(way, half, step - 1)[1].wait_recv()
                    pb[half * 2:(half + 1) * 2, d] += zb_in[way, half, step - 2]
                copy.start()
                ends.append(copy)

    zb_step(1)
    xa["far0"].wait_recv()
    pa[at_x(1), 0:4] += xa_mid[0]
    xa["sum0"].start()
    xa["far1"].wait_recv()
    pa[at_x(3), 4:8] += xa_mid[1]
    xa["sum1"].start()
    zb_step(2)
    zb_step(3)
    for name in ("near1", "near0", "sum0", "sum1"):
        xa[name].wait_recv()
    for half in (0, 1):
        rows = slice(half * 4, half * 4 + 4)
        za[rows] = pa[x, rows] + xa_fin[0, half] + xa_fin[1, half]

    def xb_copy(k):
        return remote(
            sb.at[at_x(k)], xb_in.at[k], xb_send.at[k], xb_recv.at[k], (at_x(k) * NZ + z, q)
        )

    def za_copy(k):
        return remote(
            za.at[at_z(k)], za_in.at[k], za_send.at[k], za_recv.at[k], (x * NZ + at_z(k), q)
        )

    to_col = 2 * z + 1 - lax.rem(x, 2)

    def hand_over(rows, into, parity, send, recv):
        return remote(
            rows.at[parity], into.at[x // 2], send.at[parity], recv.at[0],
            (q + 16 * parity, to_col),
        )

    for k in (4, 3, 5, 2, 6, 1, 7):
        za_copy(k).start()
    zb_step(4)
    for half in (0, 1):
        last = [steps_of(way, half) for way in (0, 1)]
        for way in (0, 1):
            zb_copy(way, half, last[way])[1].wait_recv()
        rows = slice(half * 2, half * 2 + 2)
        sb[rows] = pb[rows, z] + zb_in[0, half, last[0] - 1] + zb_in[1, half, last[1] - 1]
    for k in (2, 1, 3):
        xb_copy(k).start()

    for k in range(1, NZ):
        za_copy(k).wait_recv()
    value = za[z]
    for k in range(1, NZ):
        value = value + za_in[k]
    for c in range(8):
        block = value[c // 2, c % 2] * (-col_mask(s1, c))
        out_a[c] = block
        rows_1[c % 2, c // 2] = block
    for parity in (0, 1):
        hand_over(rows_1, ex_a, parity, exa_send, exa_recv).start()
    for k in range(1, NX):
        xb_copy(k).wait_recv()
    value = sb[x] + xb_in[1] + xb_in[2] + xb_in[3]
    for c in range(8):
        block = value[c // 2, c % 2] * (-col_mask(s2, c))
        out_b[c] = block
        rows_2[c % 2, c // 2] = block
    for parity in (0, 1):
        hand_over(rows_2, ex_b, parity, exb_send, exb_recv).start()

    def at_sum(m, j):
        return j * NZ + lax.rem(y + 3 * m, NZ)

    def tile_copy(m, j):
        return remote(
            pt.at[m, j], rr.at[p], rr_send.at[m, j], rr_recv.at[0], (at_sum(m, j), q)
        )

    def panel_rows(ref):
        return split(jnp.concatenate([ref[:, r].reshape(16, 128) for r in range(4)], axis=1))

    def send_tiles(m, value):
        for s in range(2):
            for h in range(2):
                pt[m, s * 2 + h] = value[s * 8:(s + 1) * 8, h * 128:(h + 1) * 128]
        for j in range(4):
            @pl.when(at_sum(m, j) != p)
            def _():
                tile_copy(m, j).start()

            @pl.when(at_sum(m, j) == p)
            def _():
                pltpu.make_async_copy(pt.at[m, j], rr.at[p], rr_recv.at[0]).start()

    pltpu.make_async_copy(ex_a, ex_a, exa_recv.at[0]).wait()
    rows_a = panel_rows(ex_a)
    send_tiles(0, dot3(rows_a, (p_hi[0], p_lo[0]), NT))
    send_tiles(1, dot3(rows_a, (p_hi[1], p_lo[1]), NT))
    pltpu.make_async_copy(ex_b, ex_b, exb_recv.at[0]).wait()
    rows_b = panel_rows(ex_b)
    send_tiles(2, dot3(rows_b, (p_hi[1], p_lo[1]), NT))

    turn = lax.rem(z - y + NZ, NZ)
    mine = turn // 3

    def make_sums(which):
        @pl.when(which)
        def _():
            pltpu.make_async_copy(rr, rr, rr_recv.at[0]).wait()
            tile[...] = jnp.sum(rr[...], axis=0)
            place = fin.at[core, x, mine, y]
            spot = yz_recv.at[mine // 2]
            pltpu.make_async_copy(tile, place, spot).start()

            def spread(k, carry):
                remote(
                    tile, place, yz_send.at[0], spot,
                    (x * NZ + at_z(k // NY), at_y(lax.rem(k, NY)) * 2 + core),
                ).start()
                return carry

            lax.fori_loop(1, NY * NZ, spread, 0)

    make_sums(jnp.logical_or(turn == 0, turn == 3))
    make_sums(turn == 6)

    def part(origin, which):
        return fin.at[core, origin, 0:2] if which == 0 else fin.at[core, origin, 2:3]

    def fx_copy(which, k):
        return remote(
            part(x, which), part(x, which), fx_send.at[which, k], fx_recv.at[which, k],
            (at_x(k) * NZ + z, q),
        )

    def fs_copy(which, k):
        ref = part(at_x(-k), which)
        return remote(ref, ref, fs_send.at[which, k], fs_recv.at[which, k], sibling)

    for which in (0, 1):
        block = part(x, which)
        pltpu.make_async_copy(block, block, yz_recv.at[which]).wait()
        for k in (2, 1, 3):
            fx_copy(which, k).start()
        fs_copy(which, 0).start()
    for which in (0, 1):
        for k in (1, 3, 2):
            fx_copy(which, k).wait_recv()
            fs_copy(which, k).start()

    loads[1].wait()
    loads[2].wait()
    for k in range(4):
        fs_copy(0, k).wait_recv()

    def places():
        for co in range(2):
            for xo in range(4):
                xs, h = (1 - co) + 2 * (xo // 2), xo % 2
                yield (
                    slice(xs * 64, xs * 64 + 64), slice(h * 128, h * 128 + 128),
                    fin.at[co, xo],
                )

    for rows, columns, ref in places():
        own_1[rows, columns] = d1[rows, columns] - ref[0].reshape(64, 128)
        cross_out[rows, columns] = ref[1].reshape(64, 128)
    cross = -(cross_out[...].T + dot3(ct_parts, split(own_1[...])))
    cross_out[...] = cross
    last = d2[...] - dot3(split(cross), c_parts)
    for k in range(4):
        fs_copy(1, k).wait_recv()
    for rows, columns, ref in places():
        own_2[rows, columns] = last[rows, columns] - ref[2].reshape(64, 128)

    for copy in ends:
        copy.wait_send()
    for k in range(1, NZ):
        cz_copy(k).wait_send()
        za_copy(k).wait_send()
    for k in range(1, NX):
        cx_copy(k).wait_send()
        xb_copy(k).wait_send()
        for which in (0, 1):
            fx_copy(which, k).wait_send()
    for k in range(4):
        for which in (0, 1):
            fs_copy(which, k).wait_send()
    for parity in (0, 1):
        hand_over(rows_1, ex_a, parity, exa_send, exa_recv).wait_send()
        hand_over(rows_2, ex_b, parity, exb_send, exb_recv).wait_send()
    for m in range(3):
        for j in range(4):
            @pl.when(at_sum(m, j) != p)
            def _():
                tile_copy(m, j).wait_send()

    @pl.when(lax.rem(turn, 3) == 0)
    def _():
        pltpu.make_async_copy(all_sent, all_sent, yz_send.at[0]).wait()


def body(
    inverse_block,
    panel_first,
    panel_second,
    coupling,
    dinv_first,
    dinv_second,
    struct_first,
    struct_second,
):
    dma = pltpu.SemaphoreType.DMA
    any_space = pl.BlockSpec(memory_space=pl.ANY)
    vmem = pl.BlockSpec(memory_space=pltpu.VMEM)
    square = jax.ShapeDtypeStruct((256, 256), F32)
    rows = jax.ShapeDtypeStruct((8, 8, 128), F32)
    row_a, own_a, row_b, cross, own_b = pl.pallas_call(
        kernel,
        out_shape=(rows, square, rows, square, square),
        in_specs=[any_space] * 8,
        out_specs=(vmem,) * 5,
        scratch_shapes=[
            pltpu.SMEM((128,), jnp.int32),
            pltpu.SMEM((128,), jnp.int32),
            pltpu.VMEM((4096, 128), F32),
            pltpu.VMEM((512, 1024), BF16),
            pltpu.VMEM((512, 1024), BF16),
            pltpu.VMEM((2, 4, 256, 128), F32),
            pltpu.VMEM((2, 256, 512), BF16),
            pltpu.VMEM((2, 256, 512), BF16),
            pltpu.VMEM((256, 256), F32),
            pltpu.VMEM((256, 256), F32),
            pltpu.VMEM((256, 256), F32),
            pltpu.VMEM((4, 8, 4, 2, 8, 128), F32),
            pltpu.VMEM((4, 8, 4, 2, 8, 128), F32),
            pltpu.VMEM((8, 4, 2, 8, 128), F32),
            pltpu.VMEM((4, 4, 2, 8, 128), F32),
            pltpu.VMEM((2, 4, 4, 2, 8, 128), F32),
            pltpu.VMEM((2, 2, 4, 4, 2, 8, 128), F32),
            pltpu.VMEM((4, 4, 2, 8, 128), F32),
            pltpu.VMEM((8, 4, 2, 8, 128), F32),
            pltpu.VMEM((2, 2, 4, 2, 4, 2, 8, 128), F32),
            pltpu.VMEM((2, 4, 8, 128), F32),
            pltpu.VMEM((2, 4, 8, 128), F32),
            pltpu.VMEM((2, 4, 8, 128), F32),
            pltpu.VMEM((2, 4, 8, 128), F32),
            pltpu.VMEM((3, 4, 8, 128), F32),
            pltpu.VMEM((32, 8, 128), F32),
            pltpu.VMEM((8, 128), F32),
            pltpu.VMEM((2, 4, 3, 8, 8, 128), F32),
            pltpu.VMEM((63, 8, 128), F32),
            dma((5,)), dma((3,)),
            dma((2, 9)), dma((2, 9)), dma((2, 9)), dma((2, 9)),
            dma((8,)), dma((8,)), dma((4,)), dma((4,)),
            dma((6,)), dma((6,)), dma((4,)), dma((4,)),
            dma((8,)), dma((8,)), dma((2, 2, 4)), dma((2, 2, 4)),
            dma((2,)), dma((1,)), dma((2,)), dma((1,)),
            dma((3, 4)), dma((1,)), dma((1,)), dma((2,)),
            dma((2, 4)), dma((2, 4)), dma((2, 4)), dma((2, 4)),
        ],
        compiler_params=pltpu.CompilerParams(
            collective_id=0, has_side_effects=True, vmem_limit_bytes=60 * 1024 * 1024
        ),
        name="selected_inversion",
    )(
        inverse_block.reshape(4096, 128),
        panel_first.reshape(4, 16, 128),
        panel_second.reshape(4, 16, 128),
        coupling, dinv_first, dinv_second, struct_first, struct_second,
    )
    return (
        row_a.reshape(8, 1, 8, 128), own_a, row_b.reshape(8, 1, 8, 128), cross, own_b,
    )


def solution(mesh):
    return jax.shard_map(
        body,
        mesh=mesh,
        in_specs=(
            P(None, "prow", None, None, "pcol", None),
            P(None, "prow", "pcol", None),
            P(None, "prow", "pcol", None),
            P("prow", None),
            P(),
            P(),
            P(),
            P(),
        ),
        out_specs=(P(None, "pcol", "prow", None), P(), P(None, "pcol", "prow", None), P(), P()),
        check_vma=False,
    )
```

time: 760 us -> 91.1 us (0.12)
  waiting for transfers between devices: 644 us -> 0 us
  Pallas kernels: 0 us -> 82.4 us
  blocking collectives: 75.1 us -> 0 us
  matrix products: 15.9 us -> 0 us
  between operations: 13.9 us -> 0.64 us
    psum x5 -> x0, waiting for transfers between devices: 644 us -> none  [the longest x1 158 us: body(): column_a = lax.psum(term_a, 'prow')]
    pallas_call x0 -> x1, Pallas kernels: none -> 82.4 us  [body(): pl.pallas_call(kernel, out_shape=(rows, square, rows, square, square), in...]
    all_gather x3 -> x0, blocking collectives: 75.1 us -> none  [the longest x1 35 us: body(): coupling_full = lax.all_gather(coupling, 'prow', axis=0, tiled=True)]
    dot_general x8 -> x0, matrix products: 15.9 us -> none  [the longest x2 6.26 us: product(): return jnp.einsum('rwx,rxcy->cwy', panel * mask, local, precision=highest)]
  transfers between devices with their start and end apart: 5 -> 0, of which waited for: 5 -> 0; matrix products, arithmetic and copies ran while one was open for 1% -> 0% of each run, Pallas kernels for 0% -> 0%
where the time goes in v2:
time: 91.1 us; the launch traced here: 90.8 us
  Pallas kernels  82.4 us (90%)
  local copies, waits for them, and re-layouts  7.75 us (9%)
    pallas_call x1, Pallas kernels, body(): pl.pallas_call(kernel, out_shape=(rows, square, rows, square, square), in...  82.4 us
    unnamed x5, local copies, waits for them, and re-layouts  7.75 us

profile of v2, /device:TPU:1, one launch (start us, length us, event | category | flops | bytes accessed | tf_op | source)
XLA Modules:
  0.0 90.8 jit_solution(17155257224114357027)
XLA Ops:
  0.6 82.4 %selected_inversion.1 = (f32[8,8,128]{2,1,0:T(8,128)}, f32[256,256]{1,0:T(8,128)}, f32[8,8,128]{2,1,0:T(8,128)}, f32[256,256]{1,0:T(8,128)}, f32[256,256]{1,0:T(8,128)}) custom-call(f32[4096,128]{1,0:T(8,128)} %bitcast.9, f32[4,16,128]{2,1,0:T(8,128)} %bitcast.10, f32[4,16,128]{2,1,0:T(8,128)} %bitcast.11, f32[8,256]{1,0:T(8,128)} %c_hbm.1, ...), custom_call_target="tpu_custom_call" | custom-call | tf_op jit(solution)/shard_map/selected_inversion/pallas_call | solution.py:476
  83.0 1.4 %copy.20 = f32[8,1,8,128]{3,2,1,0:T(8,128)} copy(f32[8,1,8,128]{3,2,1,0:T(8,128)} %bitcast.13) | data formatting | bytes 65536
  84.4 1.7 %copy.21 = f32[256,256]{1,0:T(8,128)} copy(f32[256,256]{1,0:T(8,128)} %get-tuple-element.26) | data formatting | bytes 524288
  86.1 1.4 %copy.22 = f32[8,1,8,128]{3,2,1,0:T(8,128)} copy(f32[8,1,8,128]{3,2,1,0:T(8,128)} %bitcast.12) | data formatting | bytes 65536
  87.4 1.7 %copy.23 = f32[256,256]{1,0:T(8,128)} copy(f32[256,256]{1,0:T(8,128)} %get-tuple-element.28) | data formatting | bytes 524288
  89.1 1.7 %copy.24 = f32[256,256]{1,0:T(8,128)} copy(f32[256,256]{1,0:T(8,128)} %get-tuple-element.29) | data formatting | bytes 524288

commit v3 on v2

--- a/solution.py
+++ b/solution.py
@@ -64,6 +64,13 @@
             device_id=where, device_id_type=MESH,
         )
 
+    barrier = pltpu.get_barrier_semaphore()
+    near = [(p, at_y(k) * 2 + core) for k in (1, -1, 2, -2)] + [sibling]
+    near += [(x * NZ + at_z(k), q) for k in range(1, NZ)]
+    near += [(at_x(k) * NZ + z, q) for k in range(1, NX)]
+    for where in near:
+        pl.semaphore_signal(barrier, inc=1, device_id=where, device_id_type=MESH)
+
     rows16 = pl.ds(pl.multiple_of(q * 16, 16), 16)
     rows8 = pl.ds(pl.multiple_of(p * 8, 8), 8)
     own = [
@@ -81,16 +88,7 @@
     for copy in own + loads:
         copy.start()
 
-    barrier = pltpu.get_barrier_semaphore()
-    near = [(p, at_y(k) * 2 + core) for k in (1, -1, 2, -2)] + [sibling]
-    near += [(x * NZ + at_z(k), q) for k in range(1, NZ)]
-    near += [(at_x(k) * NZ + z, q) for k in range(1, NX)]
-    for where in near:
-        pl.semaphore_signal(barrier, inc=1, device_id=where, device_id_type=MESH)
     pl.semaphore_wait(barrier, len(near))
-
-    for copy in own:
-        copy.wait()
 
     ends = []
 
@@ -123,10 +121,14 @@
         ring(k, of, 0).wait_recv()
         across(k, of)
 
-    for k in (0, 1):
-        for to in (2, -2, 1, -1):
-            push(k, 0, to)
-        across(k, 0)
+    own[0].wait()
+    for to in (2, -2, 1, -1):
+        push(0, 0, to)
+    across(0, 0)
+    own[1].wait()
+    for to in (2, -2):
+        push(1, 0, to)
+    own[2].wait()
 
     def cz_copy(k):
         return remote(
@@ -149,16 +151,21 @@
 
     lax.fori_loop(0, 8, split_g, 0)
 
-    for k in (0, 1):
-        for of in (-2, 2):
-            got(k, of)
-            way = 1 if of < 0 else -1
-            push(k, of, way)
-            if (of < 0) == (k == 0):
-                push(k, of, 2 * way)
-        got(k, -1)
-        got(k, 1)
-
+    def forward(k, of):
+        ring(k, of, 0).wait_recv()
+        way = 1 if of < 0 else -1
+        push(k, of, way)
+        if (of < 0) == (k == 0):
+            push(k, of, 2 * way)
+        across(k, of)
+
+    forward(0, -2)
+    forward(0, 2)
+    for to in (1, -1):
+        push(1, 0, to)
+    across(1, 0)
+    got(0, -1)
+    got(0, 1)
     for k in range(1, NZ):
         cz_copy(k).wait_recv()
     rows64 = pl.ds(pl.multiple_of(x * 64, 64), 64)
@@ -171,10 +178,13 @@
 
     for k in range(1, NX):
         cx_copy(k).start()
+    got(0, -3)
+    got(0, 3)
+    forward(1, -2)
+    forward(1, 2)
+    got(0, -4)
 
     def prepare(k, struct):
-        for of in (-3, 3, -4 if k == 0 else 4):
-            got(k, of)
         for copy in crossing[k]:
             copy.wait_recv()
         for r in range(4):
@@ -217,6 +227,8 @@
         xa[name].start()
     ends.extend(xa.values())
 
+    for of in (-1, 1, -3, 3, 4):
+        got(1, of)
     for k in range(1, NX):
         cx_copy(k).wait_recv()
     coupling = c_full[...]
@@ -238,25 +250,25 @@
 
     lax.fori_loop(0, 4, mul_b, 0)
 
-    def zb_copy(way, half, step):
-        away = steps_of(way, half) - step + 1
+    def zb_copy(way, j, step):
+        away = steps_of(way, j // 2) - step + 1
         d = at_z(away) if way == 0 else at_z(-away)
         to_z = at_z(1) if way == 0 else at_z(-1)
         return d, remote(
-            pb.at[half * 2:(half + 1) * 2, d], zb_in.at[way, half, step - 1],
-            zb_send.at[way, half, step - 1], zb_recv.at[way, half, step - 1],
+            pb.at[j, d], zb_in.at[way, j, step - 1],
+            zb_send.at[way, j, step - 1], zb_recv.at[way, j, step - 1],
             (x * NZ + to_z, q),
         )
 
     def zb_step(step):
-        for half in (0, 1):
+        for j in range(4):
             for way in (0, 1):
-                if step > steps_of(way, half):
+                if step > steps_of(way, j // 2):
                     continue
-                d, copy = zb_copy(way, half, step)
+                d, copy = zb_copy(way, j, step)
                 if step > 1:
-                    zb_copy(way, half, step - 1)[1].wait_recv()
-                    pb[half * 2:(half + 1) * 2, d] += zb_in[way, half, step - 2]
+                    zb_copy(way, j, step - 1)[1].wait_recv()
+                    pb[j, d] += zb_in[way, j, step - 2]
                 copy.start()
                 ends.append(copy)
 
@@ -296,12 +308,11 @@
     for k in (4, 3, 5, 2, 6, 1, 7):
         za_copy(k).start()
     zb_step(4)
-    for half in (0, 1):
-        last = [steps_of(way, half) for way in (0, 1)]
+    for j in range(4):
+        last = [steps_of(way, j // 2) for way in (0, 1)]
         for way in (0, 1):
-            zb_copy(way, half, last[way])[1].wait_recv()
-        rows = slice(half * 2, half * 2 + 2)
-        sb[rows] = pb[rows, z] + zb_in[0, half, last[0] - 1] + zb_in[1, half, last[1] - 1]
+            zb_copy(way, j, last[way])[1].wait_recv()
+        sb[j] = pb[j, z] + zb_in[0, j, last[0] - 1] + zb_in[1, j, last[1] - 1]
     for k in (2, 1, 3):
         xb_copy(k).start()
 
@@ -367,7 +378,7 @@
             pltpu.make_async_copy(rr, rr, rr_recv.at[0]).wait()
             tile[...] = jnp.sum(rr[...], axis=0)
             place = fin.at[core, x, mine, y]
-            spot = yz_recv.at[mine // 2]
+            spot = yz_recv.at[mine]
             pltpu.make_async_copy(tile, place, spot).start()
 
             def spread(k, carry):
@@ -383,7 +394,7 @@
     make_sums(turn == 6)
 
     def part(origin, which):
-        return fin.at[core, origin, 0:2] if which == 0 else fin.at[core, origin, 2:3]
+        return fin.at[core, origin, which]
 
     def fx_copy(which, k):
         return remote(
@@ -395,13 +406,13 @@
         ref = part(at_x(-k), which)
         return remote(ref, ref, fs_send.at[which, k], fs_recv.at[which, k], sibling)
 
-    for which in (0, 1):
+    for which in range(3):
         block = part(x, which)
         pltpu.make_async_copy(block, block, yz_recv.at[which]).wait()
         for k in (2, 1, 3):
             fx_copy(which, k).start()
         fs_copy(which, 0).start()
-    for which in (0, 1):
+    for which in range(3):
         for k in (1, 3, 2):
             fx_copy(which, k).wait_recv()
             fs_copy(which, k).start()
@@ -410,6 +421,7 @@
     loads[2].wait()
     for k in range(4):
         fs_copy(0, k).wait_recv()
+        fs_copy(1, k).wait_recv()
 
     def places():
         for co in range(2):
@@ -427,7 +439,7 @@
     cross_out[...] = cross
     last = d2[...] - dot3(split(cross), c_parts)
     for k in range(4):
-        fs_copy(1, k).wait_recv()
+        fs_copy(2, k).wait_recv()
     for rows, columns, ref in places():
         own_2[rows, columns] = last[rows, columns] - ref[2].reshape(64, 128)
 
@@ -439,10 +451,10 @@
     for k in range(1, NX):
         cx_copy(k).wait_send()
         xb_copy(k).wait_send()
-        for which in (0, 1):
+        for which in range(3):
             fx_copy(which, k).wait_send()
     for k in range(4):
-        for which in (0, 1):
+        for which in range(3):
             fs_copy(which, k).wait_send()
     for parity in (0, 1):
         hand_over(rows_1, ex_a, parity, exa_send, exa_recv).wait_send()
@@ -498,7 +510,7 @@
             pltpu.VMEM((2, 2, 4, 4, 2, 8, 128), F32),
             pltpu.VMEM((4, 4, 2, 8, 128), F32),
             pltpu.VMEM((8, 4, 2, 8, 128), F32),
-            pltpu.VMEM((2, 2, 4, 2, 4, 2, 8, 128), F32),
+            pltpu.VMEM((2, 4, 4, 4, 2, 8, 128), F32),
             pltpu.VMEM((2, 4, 8, 128), F32),
             pltpu.VMEM((2, 4, 8, 128), F32),
             pltpu.VMEM((2, 4, 8, 128), F32),
@@ -512,10 +524,10 @@
             dma((2, 9)), dma((2, 9)), dma((2, 9)), dma((2, 9)),
             dma((8,)), dma((8,)), dma((4,)), dma((4,)),
             dma((6,)), dma((6,)), dma((4,)), dma((4,)),
-            dma((8,)), dma((8,)), dma((2, 2, 4)), dma((2, 2, 4)),
+            dma((8,)), dma((8,)), dma((2, 4, 4)), dma((2, 4, 4)),
             dma((2,)), dma((1,)), dma((2,)), dma((1,)),
-            dma((3, 4)), dma((1,)), dma((1,)), dma((2,)),
-            dma((2, 4)), dma((2, 4)), dma((2, 4)), dma((2, 4)),
+            dma((3, 4)), dma((1,)), dma((1,)), dma((3,)),
+            dma((3, 4)), dma((3, 4)), dma((3, 4)), dma((3, 4)),
         ],
         compiler_params=pltpu.CompilerParams(
             collective_id=0, has_side_effects=True, vmem_limit_bytes=60 * 1024 * 1024

time: 91.1 us -> 91.3 us (level)
  no operation moved by 1% of the time
where the time goes in v3:
time: 91.3 us; the launch traced here: 90.9 us
  Pallas kernels  82.5 us (90%)
  local copies, waits for them, and re-layouts  7.75 us (8%)
    pallas_call x1, Pallas kernels, body(): pl.pallas_call(kernel, out_shape=(rows, square, rows, square, square), in...  82.5 us
    unnamed x5, local copies, waits for them, and re-layouts  7.75 us

profile of v3, /device:TPU:1, one launch (start us, length us, event | category | flops | bytes accessed | tf_op | source)
XLA Modules:
  0.0 90.9 jit_solution(6094954137665159275)
XLA Ops:
  0.6 82.5 %selected_inversion.1 = (f32[8,8,128]{2,1,0:T(8,128)}, f32[256,256]{1,0:T(8,128)}, f32[8,8,128]{2,1,0:T(8,128)}, f32[256,256]{1,0:T(8,128)}, f32[256,256]{1,0:T(8,128)}) custom-call(f32[4096,128]{1,0:T(8,128)} %bitcast.9, f32[4,16,128]{2,1,0:T(8,128)} %bitcast.10, f32[4,16,128]{2,1,0:T(8,128)} %bitcast.11, f32[8,256]{1,0:T(8,128)} %c_hbm.1, ...), custom_call_target="tpu_custom_call" | custom-call | tf_op jit(solution)/shard_map/selected_inversion/pallas_call | solution.py:488
  83.2 1.4 %copy.20 = f32[8,1,8,128]{3,2,1,0:T(8,128)} copy(f32[8,1,8,128]{3,2,1,0:T(8,128)} %bitcast.13) | data formatting | bytes 65536
  84.5 1.7 %copy.21 = f32[256,256]{1,0:T(8,128)} copy(f32[256,256]{1,0:T(8,128)} %get-tuple-element.26) | data formatting | bytes 524288
  86.2 1.4 %copy.22 = f32[8,1,8,128]{3,2,1,0:T(8,128)} copy(f32[8,1,8,128]{3,2,1,0:T(8,128)} %bitcast.12) | data formatting | bytes 65536
  87.6 1.7 %copy.23 = f32[256,256]{1,0:T(8,128)} copy(f32[256,256]{1,0:T(8,128)} %get-tuple-element.28) | data formatting | bytes 524288
  89.3 1.7 %copy.24 = f32[256,256]{1,0:T(8,128)} copy(f32[256,256]{1,0:T(8,128)} %get-tuple-element.29) | data formatting | bytes 524288

commit v4 on v3

--- a/solution.py
+++ b/solution.py
@@ -166,6 +166,8 @@
     across(1, 0)
     got(0, -1)
     got(0, 1)
+    forward(1, -2)
+    forward(1, 2)
     for k in range(1, NZ):
         cz_copy(k).wait_recv()
     rows64 = pl.ds(pl.multiple_of(x * 64, 64), 64)
@@ -180,8 +182,6 @@
         cx_copy(k).start()
     got(0, -3)
     got(0, 3)
-    forward(1, -2)
-    forward(1, 2)
     got(0, -4)
 
     def prepare(k, struct):
@@ -207,10 +207,59 @@
 
     lax.fori_loop(0, 4, mul_a, 0)
 
+    def zb_copy(way, j, step):
+        away = steps_of(way, j // 2) - step + 1
+        d = at_z(away) if way == 0 else at_z(-away)
+        to_z = at_z(1) if way == 0 else at_z(-1)
+        mine = pa.at[j, d] if step == 1 else zb_in.at[way, j, step - 2]
+        return d, remote(
+            mine, zb_in.at[way, j, step - 1],
+            zb_send.at[way, j, step - 1], zb_recv.at[way, j, step - 1],
+            (x * NZ + to_z, q),
+        )
+
+    def zb_step(step):
+        for j in range(4):
+            for way in (0, 1):
+                if step > steps_of(way, j // 2):
+                    continue
+                d, copy = zb_copy(way, j, step)
+                if step > 1:
+                    zb_copy(way, j, step - 1)[1].wait_recv()
+                    zb_in[way, j, step - 2] += pa[j, d]
+                copy.start()
+                ends.append(copy)
+
+    zb_step(1)
+
+    for of in (-1, 1, -3, 3, 4):
+        got(1, of)
+    zb_step(2)
+    for k in range(1, NX):
+        cx_copy(k).wait_recv()
+    coupling = c_full[...]
+    c_parts = split(coupling)
+    ct_parts = split(coupling.T)
+
+    prepare(1, s2)
+
+    def mul_b(t, carry):
+        columns = pl.ds(pl.multiple_of(t * 256, 256), 256)
+        r = dot3((p_hi[1], p_lo[1]), (g_hi[:, columns], g_lo[:, columns]))
+        first = jnp.concatenate(
+            [pa[:, :, t, h].reshape(256, 128) * col_mask(s1, 2 * t + h) for h in (0, 1)], axis=1
+        )
+        r = r - dot3(ct_parts, split(first))
+        pb[:, :, t, 0] = r[:, :128].reshape(NX, NZ, 8, 128)
+        pb[:, :, t, 1] = r[:, 128:].reshape(NX, NZ, 8, 128)
+        return carry
+
+    lax.fori_loop(0, 4, mul_b, 0)
+
     x_right, x_left = (at_x(1) * NZ + z, q), (at_x(-1) * NZ + z, q)
 
     def xa_piece(d, half):
-        return pa.at[d, half * 4:(half + 1) * 4]
+        return pb.at[d, half * 4:(half + 1) * 4]
 
     def xa_copy(index, d, half, into, where):
         return remote(xa_piece(d, half), into, xa_send.at[index], xa_recv.at[index], where)
@@ -226,116 +275,67 @@
     for name in ("far0", "far1", "near1", "near0"):
         xa[name].start()
     ends.extend(xa.values())
-
-    for of in (-1, 1, -3, 3, 4):
-        got(1, of)
-    for k in range(1, NX):
-        cx_copy(k).wait_recv()
-    coupling = c_full[...]
-    c_parts = split(coupling)
-    ct_parts = split(coupling.T)
-
-    prepare(1, s2)
-
-    def mul_b(t, carry):
-        columns = pl.ds(pl.multiple_of(t * 256, 256), 256)
-        r = dot3((p_hi[1], p_lo[1]), (g_hi[:, columns], g_lo[:, columns]))
-        first = jnp.concatenate(
-            [pa[:, :, t, h].reshape(256, 128) * col_mask(s1, 2 * t + h) for h in (0, 1)], axis=1
-        )
-        r = r - dot3(ct_parts, split(first))
-        pb[:, :, t, 0] = r[:, :128].reshape(NX, NZ, 8, 128)
-        pb[:, :, t, 1] = r[:, 128:].reshape(NX, NZ, 8, 128)
-        return carry
-
-    lax.fori_loop(0, 4, mul_b, 0)
-
-    def zb_copy(way, j, step):
-        away = steps_of(way, j // 2) - step + 1
-        d = at_z(away) if way == 0 else at_z(-away)
-        to_z = at_z(1) if way == 0 else at_z(-1)
-        return d, remote(
-            pb.at[j, d], zb_in.at[way, j, step - 1],
-            zb_send.at[way, j, step - 1], zb_recv.at[way, j, step - 1],
-            (x * NZ + to_z, q),
-        )
-
-    def zb_step(step):
-        for j in range(4):
-            for way in (0, 1):
-                if step > steps_of(way, j // 2):
-                    continue
-                d, copy = zb_copy(way, j, step)
-                if step > 1:
-                    zb_copy(way, j, step - 1)[1].wait_recv()
-                    pb[j, d] += zb_in[way, j, step - 2]
-                copy.start()
-                ends.append(copy)
-
-    zb_step(1)
+    zb_step(3)
     xa["far0"].wait_recv()
-    pa[at_x(1), 0:4] += xa_mid[0]
+    pb[at_x(1), 0:4] += xa_mid[0]
     xa["sum0"].start()
     xa["far1"].wait_recv()
-    pa[at_x(3), 4:8] += xa_mid[1]
+    pb[at_x(3), 4:8] += xa_mid[1]
     xa["sum1"].start()
-    zb_step(2)
-    zb_step(3)
-    for name in ("near1", "near0", "sum0", "sum1"):
-        xa[name].wait_recv()
-    for half in (0, 1):
-        rows = slice(half * 4, half * 4 + 4)
-        za[rows] = pa[x, rows] + xa_fin[0, half] + xa_fin[1, half]
-
-    def xb_copy(k):
-        return remote(
-            sb.at[at_x(k)], xb_in.at[k], xb_send.at[k], xb_recv.at[k], (at_x(k) * NZ + z, q)
-        )
-
-    def za_copy(k):
-        return remote(
-            za.at[at_z(k)], za_in.at[k], za_send.at[k], za_recv.at[k], (x * NZ + at_z(k), q)
-        )
-
-    to_col = 2 * z + 1 - lax.rem(x, 2)
-
-    def hand_over(rows, into, parity, send, recv):
-        return remote(
-            rows.at[parity], into.at[x // 2], send.at[parity], recv.at[0],
-            (q + 16 * parity, to_col),
-        )
-
-    for k in (4, 3, 5, 2, 6, 1, 7):
-        za_copy(k).start()
     zb_step(4)
     for j in range(4):
         last = [steps_of(way, j // 2) for way in (0, 1)]
         for way in (0, 1):
             zb_copy(way, j, last[way])[1].wait_recv()
-        sb[j] = pb[j, z] + zb_in[0, j, last[0] - 1] + zb_in[1, j, last[1] - 1]
+        sb[j] = pa[j, z] + zb_in[0, j, last[0] - 1] + zb_in[1, j, last[1] - 1]
+
+    def xb_copy(k):
+        return remote(
+            sb.at[at_x(k)], xb_in.at[k], xb_send.at[k], xb_recv.at[k], (at_x(k) * NZ + z, q)
+        )
+
+    def za_copy(k):
+        return remote(
+            za.at[at_z(k)], za_in.at[k], za_send.at[k], za_recv.at[k], (x * NZ + at_z(k), q)
+        )
+
+    to_col = 2 * z + 1 - lax.rem(x, 2)
+
+    def hand_over(rows, into, parity, send, recv):
+        return remote(
+            rows.at[parity], into.at[x // 2], send.at[parity], recv.at[0],
+            (q + 16 * parity, to_col),
+        )
+
     for k in (2, 1, 3):
         xb_copy(k).start()
-
+    for name in ("near1", "near0", "sum0", "sum1"):
+        xa[name].wait_recv()
+    for half in (0, 1):
+        rows = slice(half * 4, half * 4 + 4)
+        za[rows] = pb[x, rows] + xa_fin[0, half] + xa_fin[1, half]
+    for k in (4, 3, 5, 2, 6, 1, 7):
+        za_copy(k).start()
+
+    def deliver(value, struct, out, rows, into, send, recv):
+        for c in range(8):
+            block = value[c // 2, c % 2] * (-col_mask(struct, c))
+            out[c] = block
+            rows[c % 2, c // 2] = block
+        for parity in (0, 1):
+            hand_over(rows, into, parity, send, recv).start()
+
+    for k in range(1, NX):
+        xb_copy(k).wait_recv()
+    deliver(
+        sb[x] + xb_in[1] + xb_in[2] + xb_in[3], s1, out_a, rows_1, ex_a, exa_send, exa_recv
+    )
     for k in range(1, NZ):
         za_copy(k).wait_recv()
     value = za[z]
     for k in range(1, NZ):
         value = value + za_in[k]
-    for c in range(8):
-        block = value[c // 2, c % 2] * (-col_mask(s1, c))
-        out_a[c] = block
-        rows_1[c % 2, c // 2] = block
-    for parity in (0, 1):
-        hand_over(rows_1, ex_a, parity, exa_send, exa_recv).start()
-    for k in range(1, NX):
-        xb_copy(k).wait_recv()
-    value = sb[x] + xb_in[1] + xb_in[2] + xb_in[3]
-    for c in range(8):
-        block = value[c // 2, c % 2] * (-col_mask(s2, c))
-        out_b[c] = block
-        rows_2[c % 2, c // 2] = block
-    for parity in (0, 1):
-        hand_over(rows_2, ex_b, parity, exb_send, exb_recv).start()
+    deliver(value, s2, out_b, rows_2, ex_b, exb_send, exb_recv)
 
     def at_sum(m, j):
         return j * NZ + lax.rem(y + 3 * m, NZ)
@@ -381,14 +381,17 @@
             spot = yz_recv.at[mine]
             pltpu.make_async_copy(tile, place, spot).start()
 
+            def far_first(k):
+                return 4 + (k + 1) // 2 * (1 - 2 * lax.rem(k, 2))
+
             def spread(k, carry):
+                to_z, to_y = at_z(far_first(k // NY)), at_y(far_first(lax.rem(k, NY)))
                 remote(
-                    tile, place, yz_send.at[0], spot,
-                    (x * NZ + at_z(k // NY), at_y(lax.rem(k, NY)) * 2 + core),
+                    tile, place, yz_send.at[0], spot, (x * NZ + to_z, to_y * 2 + core)
                 ).start()
                 return carry
 
-            lax.fori_loop(1, NY * NZ, spread, 0)
+            lax.fori_loop(0, NY * NZ - 1, spread, 0)
 
     make_sums(jnp.logical_or(turn == 0, turn == 3))
     make_sums(turn == 6)

time: 91.3 us -> 92.4 us (1.012)
  Pallas kernels: 82.5 us -> 83.7 us
    pallas_call x1, Pallas kernels: 82.5 us -> 83.7 us  [body(): pl.pallas_call(kernel, out_shape=(rows, square, rows, square, square), in...]
where the time goes in v4:
time: 92.4 us; the launch traced here: 92.1 us
  Pallas kernels  83.7 us (91%)
  local copies, waits for them, and re-layouts  7.75 us (8%)
    pallas_call x1, Pallas kernels, body(): pl.pallas_call(kernel, out_shape=(rows, square, rows, square, square), in...  83.7 us
    unnamed x5, local copies, waits for them, and re-layouts  7.75 us

profile of v4, /device:TPU:1, one launch (start us, length us, event | category | flops | bytes accessed | tf_op | source)
XLA Modules:
  0.0 92.1 jit_solution(16862182962381516623)
XLA Ops:
  0.6 83.7 %selected_inversion.1 = (f32[8,8,128]{2,1,0:T(8,128)}, f32[256,256]{1,0:T(8,128)}, f32[8,8,128]{2,1,0:T(8,128)}, f32[256,256]{1,0:T(8,128)}, f32[256,256]{1,0:T(8,128)}) custom-call(f32[4096,128]{1,0:T(8,128)} %bitcast.9, f32[4,16,128]{2,1,0:T(8,128)} %bitcast.10, f32[4,16,128]{2,1,0:T(8,128)} %bitcast.11, f32[8,256]{1,0:T(8,128)} %c_hbm.1, ...), custom_call_target="tpu_custom_call" | custom-call | tf_op jit(solution)/shard_map/selected_inversion/pallas_call | solution.py:491
  84.3 1.4 %copy.20 = f32[8,1,8,128]{3,2,1,0:T(8,128)} copy(f32[8,1,8,128]{3,2,1,0:T(8,128)} %bitcast.13) | data formatting | bytes 65536
  85.7 1.7 %copy.21 = f32[256,256]{1,0:T(8,128)} copy(f32[256,256]{1,0:T(8,128)} %get-tuple-element.26) | data formatting | bytes 524288
  87.4 1.4 %copy.22 = f32[8,1,8,128]{3,2,1,0:T(8,128)} copy(f32[8,1,8,128]{3,2,1,0:T(8,128)} %bitcast.12) | data formatting | bytes 65536
  88.7 1.7 %copy.23 = f32[256,256]{1,0:T(8,128)} copy(f32[256,256]{1,0:T(8,128)} %get-tuple-element.28) | data formatting | bytes 524288
  90.4 1.7 %copy.24 = f32[256,256]{1,0:T(8,128)} copy(f32[256,256]{1,0:T(8,128)} %get-tuple-element.29) | data formatting | bytes 524288

commit v5 on v3

--- a/solution.py
+++ b/solution.py
@@ -166,6 +166,8 @@
     across(1, 0)
     got(0, -1)
     got(0, 1)
+    forward(1, -2)
+    forward(1, 2)
     for k in range(1, NZ):
         cz_copy(k).wait_recv()
     rows64 = pl.ds(pl.multiple_of(x * 64, 64), 64)
@@ -180,8 +182,6 @@
         cx_copy(k).start()
     got(0, -3)
     got(0, 3)
-    forward(1, -2)
-    forward(1, 2)
     got(0, -4)
 
     def prepare(k, struct):
@@ -235,17 +235,24 @@
     c_parts = split(coupling)
     ct_parts = split(coupling.T)
 
+    def mul_c(t, carry):
+        first = jnp.concatenate(
+            [pa[:, :, t, h].reshape(256, 128) * col_mask(s1, 2 * t + h) for h in (0, 1)], axis=1
+        )
+        r = dot3(ct_parts, split(first))
+        pb[:, :, t, 0] = r[:, :128].reshape(NX, NZ, 8, 128)
+        pb[:, :, t, 1] = r[:, 128:].reshape(NX, NZ, 8, 128)
+        return carry
+
+    lax.fori_loop(0, 4, mul_c, 0)
     prepare(1, s2)
 
     def mul_b(t, carry):
         columns = pl.ds(pl.multiple_of(t * 256, 256), 256)
         r = dot3((p_hi[1], p_lo[1]), (g_hi[:, columns], g_lo[:, columns]))
-        first = jnp.concatenate(
-            [pa[:, :, t, h].reshape(256, 128) * col_mask(s1, 2 * t + h) for h in (0, 1)], axis=1
-        )
-        r = r - dot3(ct_parts, split(first))
-        pb[:, :, t, 0] = r[:, :128].reshape(NX, NZ, 8, 128)
-        pb[:, :, t, 1] = r[:, 128:].reshape(NX, NZ, 8, 128)
+        for h in (0, 1):
+            block = r[:, h * 128:(h + 1) * 128].reshape(NX, NZ, 8, 128)
+            pb[:, :, t, h] = block - pb[:, :, t, h]
         return carry
 
     lax.fori_loop(0, 4, mul_b, 0)
@@ -292,10 +299,27 @@
             sb.at[at_x(k)], xb_in.at[k], xb_send.at[k], xb_recv.at[k], (at_x(k) * NZ + z, q)
         )
 
-    def za_copy(k):
-        return remote(
-            za.at[at_z(k)], za_in.at[k], za_send.at[k], za_recv.at[k], (x * NZ + at_z(k), q)
-        )
+    def za_copy(way, half, step):
+        away = steps_of(way, half) - step + 1
+        d = at_z(away) if way == 0 else at_z(-away)
+        to_z = at_z(1) if way == 0 else at_z(-1)
+        return d, remote(
+            za.at[d, half * 2:(half + 1) * 2], za_in.at[way, half, step - 1],
+            za_send.at[way, half, step - 1], za_recv.at[way, half, step - 1],
+            (x * NZ + to_z, q),
+        )
+
+    def za_step(step):
+        for half in (0, 1):
+            for way in (0, 1):
+                if step > steps_of(way, half):
+                    continue
+                d, copy = za_copy(way, half, step)
+                if step > 1:
+                    za_copy(way, half, step - 1)[1].wait_recv()
+                    za[d, half * 2:(half + 1) * 2] += za_in[way, half, step - 2]
+                copy.start()
+                ends.append(copy)
 
     to_col = 2 * z + 1 - lax.rem(x, 2)
 
@@ -305,9 +329,10 @@
             (q + 16 * parity, to_col),
         )
 
-    for k in (4, 3, 5, 2, 6, 1, 7):
-        za_copy(k).start()
+    za_step(1)
     zb_step(4)
+    za_step(2)
+    za_step(3)
     for j in range(4):
         last = [steps_of(way, j // 2) for way in (0, 1)]
         for way in (0, 1):
@@ -316,26 +341,30 @@
     for k in (2, 1, 3):
         xb_copy(k).start()
 
-    for k in range(1, NZ):
-        za_copy(k).wait_recv()
-    value = za[z]
-    for k in range(1, NZ):
-        value = value + za_in[k]
-    for c in range(8):
-        block = value[c // 2, c % 2] * (-col_mask(s1, c))
-        out_a[c] = block
-        rows_1[c % 2, c // 2] = block
-    for parity in (0, 1):
-        hand_over(rows_1, ex_a, parity, exa_send, exa_recv).start()
+    za_step(4)
+
+    def deliver(value, c, struct, out, rows):
+        block = value * (-col_mask(struct, c))
+        out[c] = block
+        rows[c % 2, c // 2] = block
+
     for k in range(1, NX):
         xb_copy(k).wait_recv()
     value = sb[x] + xb_in[1] + xb_in[2] + xb_in[3]
     for c in range(8):
-        block = value[c // 2, c % 2] * (-col_mask(s2, c))
-        out_b[c] = block
-        rows_2[c % 2, c // 2] = block
+        deliver(value[c // 2, c % 2], c, s2, out_b, rows_2)
     for parity in (0, 1):
         hand_over(rows_2, ex_b, parity, exb_send, exb_recv).start()
+    for half in (0, 1):
+        last = [steps_of(way, half) for way in (0, 1)]
+        for way in (0, 1):
+            za_copy(way, half, last[way])[1].wait_recv()
+        value = za[z, half * 2:(half + 1) * 2]
+        value = value + za_in[0, half, last[0] - 1] + za_in[1, half, last[1] - 1]
+        for c in range(4 * half, 4 * half + 4):
+            deliver(value[c // 2 - 2 * half, c % 2], c, s1, out_a, rows_1)
+    for parity in (0, 1):
+        hand_over(rows_1, ex_a, parity, exa_send, exa_recv).start()
 
     def at_sum(m, j):
         return j * NZ + lax.rem(y + 3 * m, NZ)
@@ -381,14 +410,17 @@
             spot = yz_recv.at[mine]
             pltpu.make_async_copy(tile, place, spot).start()
 
+            def far_first(k):
+                return 4 + (k + 1) // 2 * (1 - 2 * lax.rem(k, 2))
+
             def spread(k, carry):
+                to_z, to_y = at_z(far_first(k // NY)), at_y(far_first(lax.rem(k, NY)))
                 remote(
-                    tile, place, yz_send.at[0], spot,
-                    (x * NZ + at_z(k // NY), at_y(lax.rem(k, NY)) * 2 + core),
+                    tile, place, yz_send.at[0], spot, (x * NZ + to_z, to_y * 2 + core)
                 ).start()
                 return carry
 
-            lax.fori_loop(1, NY * NZ, spread, 0)
+            lax.fori_loop(0, NY * NZ - 1, spread, 0)
 
     make_sums(jnp.logical_or(turn == 0, turn == 3))
     make_sums(turn == 6)
@@ -447,7 +479,6 @@
         copy.wait_send()
     for k in range(1, NZ):
         cz_copy(k).wait_send()
-        za_copy(k).wait_send()
     for k in range(1, NX):
         cx_copy(k).wait_send()
         xb_copy(k).wait_send()
@@ -509,7 +540,7 @@
             pltpu.VMEM((2, 4, 4, 2, 8, 128), F32),
             pltpu.VMEM((2, 2, 4, 4, 2, 8, 128), F32),
             pltpu.VMEM((4, 4, 2, 8, 128), F32),
-            pltpu.VMEM((8, 4, 2, 8, 128), F32),
+            pltpu.VMEM((2, 2, 4, 2, 2, 8, 128), F32),
             pltpu.VMEM((2, 4, 4, 4, 2, 8, 128), F32),
             pltpu.VMEM((2, 4, 8, 128), F32),
             pltpu.VMEM((2, 4, 8, 128), F32),
@@ -524,7 +555,7 @@
             dma((2, 9)), dma((2, 9)), dma((2, 9)), dma((2, 9)),
             dma((8,)), dma((8,)), dma((4,)), dma((4,)),
             dma((6,)), dma((6,)), dma((4,)), dma((4,)),
-            dma((8,)), dma((8,)), dma((2, 4, 4)), dma((2, 4, 4)),
+            dma((2, 2, 4)), dma((2, 2, 4)), dma((2, 4, 4)), dma((2, 4, 4)),
             dma((2,)), dma((1,)), dma((2,)), dma((1,)),
             dma((3, 4)), dma((1,)), dma((1,)), dma((3,)),
             dma((3, 4)), dma((3, 4)), dma((3, 4)), dma((3, 4)),

time: 91.3 us -> 92.6 us (1.014)
  Pallas kernels: 82.5 us -> 83.8 us
    pallas_call x1, Pallas kernels: 82.5 us -> 83.8 us  [body(): pl.pallas_call(kernel, out_shape=(rows, square, rows, square, square), in...]
where the time goes in v5:
time: 92.6 us; the launch traced here: 92.2 us
  Pallas kernels  83.8 us (90%)
  local copies, waits for them, and re-layouts  7.75 us (8%)
    pallas_call x1, Pallas kernels, body(): pl.pallas_call(kernel, out_shape=(rows, square, rows, square, square), in...  83.8 us
    unnamed x5, local copies, waits for them, and re-layouts  7.75 us

profile of v5, /device:TPU:1, one launch (start us, length us, event | category | flops | bytes accessed | tf_op | source)
XLA Modules:
  0.0 92.2 jit_solution(6469913532031087478)
XLA Ops:
  0.6 83.8 %selected_inversion.1 = (f32[8,8,128]{2,1,0:T(8,128)}, f32[256,256]{1,0:T(8,128)}, f32[8,8,128]{2,1,0:T(8,128)}, f32[256,256]{1,0:T(8,128)}, f32[256,256]{1,0:T(8,128)}) custom-call(f32[4096,128]{1,0:T(8,128)} %bitcast.9, f32[4,16,128]{2,1,0:T(8,128)} %bitcast.10, f32[4,16,128]{2,1,0:T(8,128)} %bitcast.11, f32[8,256]{1,0:T(8,128)} %c_hbm.1, ...), custom_call_target="tpu_custom_call" | custom-call | tf_op jit(solution)/shard_map/selected_inversion/pallas_call | solution.py:519
  84.4 1.4 %copy.20 = f32[8,1,8,128]{3,2,1,0:T(8,128)} copy(f32[8,1,8,128]{3,2,1,0:T(8,128)} %bitcast.13) | data formatting | bytes 65536
  85.8 1.7 %copy.21 = f32[256,256]{1,0:T(8,128)} copy(f32[256,256]{1,0:T(8,128)} %get-tuple-element.26) | data formatting | bytes 524288
  87.5 1.4 %copy.22 = f32[8,1,8,128]{3,2,1,0:T(8,128)} copy(f32[8,1,8,128]{3,2,1,0:T(8,128)} %bitcast.12) | data formatting | bytes 65536
  88.9 1.7 %copy.23 = f32[256,256]{1,0:T(8,128)} copy(f32[256,256]{1,0:T(8,128)} %get-tuple-element.28) | data formatting | bytes 524288
  90.5 1.7 %copy.24 = f32[256,256]{1,0:T(8,128)} copy(f32[256,256]{1,0:T(8,128)} %get-tuple-element.29) | data formatting | bytes 524288

commit v6 on v5

--- a/solution.py
+++ b/solution.py
@@ -37,10 +37,10 @@
     xa_mid, xa_fin, xb_in, za_in, zb_in,
     rows_1, rows_2, ex_a, ex_b, pt, rr, tile, fin, all_sent,
     load_sem, own_sem,
-    ag_send, ag_recv, sib_send, sib_recv, cz_send, cz_recv, cx_send, cx_recv,
-    xa_send, xa_recv, xb_send, xb_recv, za_send, za_recv, zb_send, zb_recv,
-    exa_send, exa_recv, exb_send, exb_recv, rr_send, rr_recv, yz_send, yz_recv,
-    fx_send, fx_recv, fs_send, fs_recv,
+    sent, ag_recv, sib_recv, cz_recv, cx_recv,
+    xa_recv, xb_recv, za_recv, zb_recv,
+    exa_recv, exb_recv, rr_send, rr_recv, yz_send, yz_recv,
+    fx_recv, fs_recv,
 ):
     p = lax.axis_index("prow")
     q = lax.axis_index("pcol")
@@ -70,6 +70,9 @@
     near += [(at_x(k) * NZ + z, q) for k in range(1, NX)]
     for where in near:
         pl.semaphore_signal(barrier, inc=1, device_id=where, device_id_type=MESH)
+
+    def all_of(ref, semaphore):
+        pltpu.make_async_copy(ref, ref, semaphore).wait()
 
     rows16 = pl.ds(pl.multiple_of(q * 16, 16), 16)
     rows8 = pl.ds(pl.multiple_of(p * 8, 8), 8)
@@ -90,8 +93,6 @@
 
     pl.semaphore_wait(barrier, len(near))
 
-    ends = []
-
     def shard(k, row_y):
         rows = row_y * 2 + core
         return full.at[k, :, pl.ds(pl.multiple_of(rows * 16, 16), 16)]
@@ -99,23 +100,18 @@
     def ring(k, of, to):
         ref = shard(k, at_y(of))
         return remote(
-            ref, ref, ag_send.at[k, of - to + 4], ag_recv.at[k, of - to + 4],
+            ref, ref, sent.at[0], ag_recv.at[k, of - to + 4],
             (p, at_y(to) * 2 + core),
         )
 
     def push(k, of, to):
         copy = ring(k, of, to)
         copy.start()
-        ends.append(copy)
-
-    crossing = {0: [], 1: []}
 
     def across(k, of):
         ref = shard(k, at_y(of))
-        copy = remote(ref, ref, sib_send.at[k, of + 4], sib_recv.at[k, of + 4], sibling)
+        copy = remote(ref, ref, sent.at[0], sib_recv.at[k], sibling)
         copy.start()
-        ends.append(copy)
-        crossing[k].append(copy)
 
     def got(k, of):
         ring(k, of, 0).wait_recv()
@@ -132,7 +128,7 @@
 
     def cz_copy(k):
         return remote(
-            c_full.at[rows8], c_full.at[rows8], cz_send.at[k], cz_recv.at[k],
+            c_full.at[rows8], c_full.at[rows8], sent.at[0], cz_recv.at[0],
             (x * NZ + at_z(k), q),
         )
 
@@ -168,13 +164,12 @@
     got(0, 1)
     forward(1, -2)
     forward(1, 2)
-    for k in range(1, NZ):
-        cz_copy(k).wait_recv()
+    all_of(c_full.at[0:56], cz_recv.at[0])
     rows64 = pl.ds(pl.multiple_of(x * 64, 64), 64)
 
     def cx_copy(k):
         return remote(
-            c_full.at[rows64], c_full.at[rows64], cx_send.at[k], cx_recv.at[k],
+            c_full.at[rows64], c_full.at[rows64], sent.at[0], cx_recv.at[0],
             (at_x(k) * NZ + z, q),
         )
 
@@ -185,8 +180,7 @@
     got(0, -4)
 
     def prepare(k, struct):
-        for copy in crossing[k]:
-            copy.wait_recv()
+        all_of(full.at[k, :, 0:128], sib_recv.at[k])
         for r in range(4):
             mask = struct[r * (NX * NZ) + p].astype(F32)
             hi, lo = split(full[k, r] * mask)
@@ -213,7 +207,7 @@
         return pa.at[d, half * 4:(half + 1) * 4]
 
     def xa_copy(index, d, half, into, where):
-        return remote(xa_piece(d, half), into, xa_send.at[index], xa_recv.at[index], where)
+        return remote(xa_piece(d, half), into, sent.at[1], xa_recv.at[min(index, 2)], where)
 
     xa = {
         "far0": xa_copy(0, at_x(2), 0, xa_mid.at[0], x_right),
@@ -225,12 +219,10 @@
     }
     for name in ("far0", "far1", "near1", "near0"):
         xa[name].start()
-    ends.extend(xa.values())
 
     for of in (-1, 1, -3, 3, 4):
         got(1, of)
-    for k in range(1, NX):
-        cx_copy(k).wait_recv()
+    all_of(c_full.at[0:192], cx_recv.at[0])
     coupling = c_full[...]
     c_parts = split(coupling)
     ct_parts = split(coupling.T)
@@ -263,7 +255,7 @@
         to_z = at_z(1) if way == 0 else at_z(-1)
         return d, remote(
             pb.at[j, d], zb_in.at[way, j, step - 1],
-            zb_send.at[way, j, step - 1], zb_recv.at[way, j, step - 1],
+            sent.at[1], zb_recv.at[way, j, step - 1],
             (x * NZ + to_z, q),
         )
 
@@ -277,7 +269,6 @@
                     zb_copy(way, j, step - 1)[1].wait_recv()
                     pb[j, d] += zb_in[way, j, step - 2]
                 copy.start()
-                ends.append(copy)
 
     zb_step(1)
     xa["far0"].wait_recv()
@@ -288,15 +279,14 @@
     xa["sum1"].start()
     zb_step(2)
     zb_step(3)
-    for name in ("near1", "near0", "sum0", "sum1"):
-        xa[name].wait_recv()
+    all_of(xa_fin, xa_recv.at[2])
     for half in (0, 1):
         rows = slice(half * 4, half * 4 + 4)
         za[rows] = pa[x, rows] + xa_fin[0, half] + xa_fin[1, half]
 
     def xb_copy(k):
         return remote(
-            sb.at[at_x(k)], xb_in.at[k], xb_send.at[k], xb_recv.at[k], (at_x(k) * NZ + z, q)
+            sb.at[at_x(k)], xb_in.at[k], sent.at[1], xb_recv.at[0], (at_x(k) * NZ + z, q)
         )
 
     def za_copy(way, half, step):
@@ -305,7 +295,7 @@
         to_z = at_z(1) if way == 0 else at_z(-1)
         return d, remote(
             za.at[d, half * 2:(half + 1) * 2], za_in.at[way, half, step - 1],
-            za_send.at[way, half, step - 1], za_recv.at[way, half, step - 1],
+            sent.at[1], za_recv.at[way, half, step - 1],
             (x * NZ + to_z, q),
         )
 
@@ -319,13 +309,12 @@
                     za_copy(way, half, step - 1)[1].wait_recv()
                     za[d, half * 2:(half + 1) * 2] += za_in[way, half, step - 2]
                 copy.start()
-                ends.append(copy)
 
     to_col = 2 * z + 1 - lax.rem(x, 2)
 
-    def hand_over(rows, into, parity, send, recv):
-        return remote(
-            rows.at[parity], into.at[x // 2], send.at[parity], recv.at[0],
+    def hand_over(rows, into, parity, recv):
+        return remote(
+            rows.at[parity], into.at[x // 2], sent.at[1], recv.at[0],
             (q + 16 * parity, to_col),
         )
 
@@ -348,13 +337,12 @@
         out[c] = block
         rows[c % 2, c // 2] = block
 
-    for k in range(1, NX):
-        xb_copy(k).wait_recv()
+    all_of(xb_in.at[1:4], xb_recv.at[0])
     value = sb[x] + xb_in[1] + xb_in[2] + xb_in[3]
     for c in range(8):
         deliver(value[c // 2, c % 2], c, s2, out_b, rows_2)
     for parity in (0, 1):
-        hand_over(rows_2, ex_b, parity, exb_send, exb_recv).start()
+        hand_over(rows_2, ex_b, parity, exb_recv).start()
     for half in (0, 1):
         last = [steps_of(way, half) for way in (0, 1)]
         for way in (0, 1):
@@ -364,14 +352,14 @@
         for c in range(4 * half, 4 * half + 4):
             deliver(value[c // 2 - 2 * half, c % 2], c, s1, out_a, rows_1)
     for parity in (0, 1):
-        hand_over(rows_1, ex_a, parity, exa_send, exa_recv).start()
+        hand_over(rows_1, ex_a, parity, exa_recv).start()
 
     def at_sum(m, j):
         return j * NZ + lax.rem(y + 3 * m, NZ)
 
     def tile_copy(m, j):
         return remote(
-            pt.at[m, j], rr.at[p], rr_send.at[m, j], rr_recv.at[0], (at_sum(m, j), q)
+            pt.at[m, j], rr.at[p], rr_send.at[0], rr_recv.at[0], (at_sum(m, j), q)
         )
 
     def panel_rows(ref):
@@ -430,13 +418,13 @@
 
     def fx_copy(which, k):
         return remote(
-            part(x, which), part(x, which), fx_send.at[which, k], fx_recv.at[which, k],
+            part(x, which), part(x, which), sent.at[2], fx_recv.at[which, k],
             (at_x(k) * NZ + z, q),
         )
 
     def fs_copy(which, k):
         ref = part(at_x(-k), which)
-        return remote(ref, ref, fs_send.at[which, k], fs_recv.at[which, k], sibling)
+        return remote(ref, ref, sent.at[2], fs_recv.at[which], sibling)
 
     for which in range(3):
         block = part(x, which)
@@ -451,9 +439,8 @@
 
     loads[1].wait()
     loads[2].wait()
-    for k in range(4):
-        fs_copy(0, k).wait_recv()
-        fs_copy(1, k).wait_recv()
+    for which in (0, 1):
+        all_of(fin.at[1 - core, :, which], fs_recv.at[which])
 
     def places():
         for co in range(2):
@@ -470,35 +457,22 @@
     cross = -(cross_out[...].T + dot3(ct_parts, split(own_1[...])))
     cross_out[...] = cross
     last = d2[...] - dot3(split(cross), c_parts)
-    for k in range(4):
-        fs_copy(2, k).wait_recv()
+    all_of(fin.at[1 - core, :, 2], fs_recv.at[2])
     for rows, columns, ref in places():
         own_2[rows, columns] = last[rows, columns] - ref[2].reshape(64, 128)
 
-    for copy in ends:
-        copy.wait_send()
-    for k in range(1, NZ):
-        cz_copy(k).wait_send()
-    for k in range(1, NX):
-        cx_copy(k).wait_send()
-        xb_copy(k).wait_send()
-        for which in range(3):
-            fx_copy(which, k).wait_send()
-    for k in range(4):
-        for which in range(3):
-            fs_copy(which, k).wait_send()
-    for parity in (0, 1):
-        hand_over(rows_1, ex_a, parity, exa_send, exa_recv).wait_send()
-        hand_over(rows_2, ex_b, parity, exb_send, exb_recv).wait_send()
-    for m in range(3):
-        for j in range(4):
-            @pl.when(at_sum(m, j) != p)
-            def _():
-                tile_copy(m, j).wait_send()
+    all_of(all_sent.at[0:302], sent.at[0])
+    all_of(all_sent, sent.at[1])
+    all_of(all_sent.at[0:168], sent.at[2])
 
     @pl.when(lax.rem(turn, 3) == 0)
     def _():
-        pltpu.make_async_copy(all_sent, all_sent, yz_send.at[0]).wait()
+        all_of(all_sent.at[0:11], rr_send.at[0])
+        all_of(all_sent.at[0:63], yz_send.at[0])
+
+    @pl.when(lax.rem(turn, 3) != 0)
+    def _():
+        all_of(all_sent.at[0:12], rr_send.at[0])
 
 
 def body(
@@ -550,15 +524,12 @@
             pltpu.VMEM((32, 8, 128), F32),
             pltpu.VMEM((8, 128), F32),
             pltpu.VMEM((2, 4, 3, 8, 8, 128), F32),
-            pltpu.VMEM((63, 8, 128), F32),
+            pltpu.VMEM((512, 8, 128), F32),
             dma((5,)), dma((3,)),
-            dma((2, 9)), dma((2, 9)), dma((2, 9)), dma((2, 9)),
-            dma((8,)), dma((8,)), dma((4,)), dma((4,)),
-            dma((6,)), dma((6,)), dma((4,)), dma((4,)),
-            dma((2, 2, 4)), dma((2, 2, 4)), dma((2, 4, 4)), dma((2, 4, 4)),
-            dma((2,)), dma((1,)), dma((2,)), dma((1,)),
-            dma((3, 4)), dma((1,)), dma((1,)), dma((3,)),
-            dma((3, 4)), dma((3, 4)), dma((3, 4)), dma((3, 4)),
+            dma((3,)), dma((2, 9)), dma((2,)), dma((1,)), dma((1,)),
+            dma((3,)), dma((1,)), dma((2, 2, 4)), dma((2, 4, 4)),
+            dma((1,)), dma((1,)), dma((1,)), dma((1,)), dma((1,)), dma((3,)),
+            dma((3, 4)), dma((3,)),
         ],
         compiler_params=pltpu.CompilerParams(
             collective_id=0, has_side_effects=True, vmem_limit_bytes=60 * 1024 * 1024

time: 92.6 us -> 90.7 us (0.979)
  Pallas kernels: 83.8 us -> 81.9 us
    pallas_call x1, Pallas kernels: 83.8 us -> 81.9 us  [body(): pl.pallas_call(kernel, out_shape=(rows, square, rows, square, square), in...]
where the time goes in v6:
time: 90.7 us; the launch traced here: 90.3 us
  Pallas kernels  81.9 us (90%)
  local copies, waits for them, and re-layouts  7.75 us (9%)
    pallas_call x1, Pallas kernels, body(): pl.pallas_call(kernel, out_shape=(rows, square, rows, square, square), in...  81.9 us
    unnamed x5, local copies, waits for them, and re-layouts  7.75 us

profile of v6, /device:TPU:1, one launch (start us, length us, event | category | flops | bytes accessed | tf_op | source)
XLA Modules:
  0.0 90.3 jit_solution(13448378332202557323)
XLA Ops:
  0.6 81.9 %selected_inversion.1 = (f32[8,8,128]{2,1,0:T(8,128)}, f32[256,256]{1,0:T(8,128)}, f32[8,8,128]{2,1,0:T(8,128)}, f32[256,256]{1,0:T(8,128)}, f32[256,256]{1,0:T(8,128)}) custom-call(f32[4096,128]{1,0:T(8,128)} %bitcast.9, f32[4,16,128]{2,1,0:T(8,128)} %bitcast.10, f32[4,16,128]{2,1,0:T(8,128)} %bitcast.11, f32[8,256]{1,0:T(8,128)} %c_hbm.1, ...), custom_call_target="tpu_custom_call" | custom-call | tf_op jit(solution)/shard_map/selected_inversion/pallas_call | solution.py:493
  82.6 1.4 %copy.20 = f32[8,1,8,128]{3,2,1,0:T(8,128)} copy(f32[8,1,8,128]{3,2,1,0:T(8,128)} %bitcast.13) | data formatting | bytes 65536
  84.0 1.7 %copy.21 = f32[256,256]{1,0:T(8,128)} copy(f32[256,256]{1,0:T(8,128)} %get-tuple-element.26) | data formatting | bytes 524288
  85.6 1.4 %copy.22 = f32[8,1,8,128]{3,2,1,0:T(8,128)} copy(f32[8,1,8,128]{3,2,1,0:T(8,128)} %bitcast.12) | data formatting | bytes 65536
  87.0 1.7 %copy.23 = f32[256,256]{1,0:T(8,128)} copy(f32[256,256]{1,0:T(8,128)} %get-tuple-element.28) | data formatting | bytes 524288
  88.7 1.7 %copy.24 = f32[256,256]{1,0:T(8,128)} copy(f32[256,256]{1,0:T(8,128)} %get-tuple-element.29) | data formatting | bytes 524288

commit v7 on v6

--- a/solution.py
+++ b/solution.py
@@ -289,26 +289,34 @@
             sb.at[at_x(k)], xb_in.at[k], sent.at[1], xb_recv.at[0], (at_x(k) * NZ + z, q)
         )
 
-    def za_copy(way, half, step):
-        away = steps_of(way, half) - step + 1
-        d = at_z(away) if way == 0 else at_z(-away)
-        to_z = at_z(1) if way == 0 else at_z(-1)
-        return d, remote(
-            za.at[d, half * 2:(half + 1) * 2], za_in.at[way, half, step - 1],
-            sent.at[1], za_recv.at[way, half, step - 1],
-            (x * NZ + to_z, q),
-        )
-
-    def za_step(step):
-        for half in (0, 1):
-            for way in (0, 1):
-                if step > steps_of(way, half):
+    def za_copy(way, half, index):
+        away, over = ((4, 2), (3, 2), (2, 2), (1, 1))[index]
+        sign = 1 - 2 * way
+        return remote(
+            za.at[at_z(sign * away), half * 2:(half + 1) * 2], za_in.at[way, half, index],
+            sent.at[1], za_recv.at[way, half, index], (x * NZ + at_z(sign * over), q),
+        )
+
+    sides = [(way, half) for half in (0, 1) for way in (0, 1)]
+
+    def za_start():
+        for way, half in sides:
+            if steps_of(way, half) == 4:
+                za_copy(way, half, 0).start()
+            za_copy(way, half, 1).start()
+        for way, half in sides:
+            if steps_of(way, half) == 3:
+                za_copy(way, half, 2).start()
+
+    def za_middle():
+        for way, half in sides:
+            for index in (0, 1):
+                if index == 0 and steps_of(way, half) == 3:
                     continue
-                d, copy = za_copy(way, half, step)
-                if step > 1:
-                    za_copy(way, half, step - 1)[1].wait_recv()
-                    za[d, half * 2:(half + 1) * 2] += za_in[way, half, step - 2]
-                copy.start()
+                za_copy(way, half, index).wait_recv()
+                d = at_z((2 - index) * (1 - 2 * way))
+                za[d, half * 2:(half + 1) * 2] += za_in[way, half, index]
+                za_copy(way, half, index + 2).start()
 
     to_col = 2 * z + 1 - lax.rem(x, 2)
 
@@ -318,10 +326,9 @@
             (q + 16 * parity, to_col),
         )
 
-    za_step(1)
+    za_start()
     zb_step(4)
-    za_step(2)
-    za_step(3)
+    za_middle()
     for j in range(4):
         last = [steps_of(way, j // 2) for way in (0, 1)]
         for way in (0, 1):
@@ -330,29 +337,28 @@
     for k in (2, 1, 3):
         xb_copy(k).start()
 
-    za_step(4)
 
     def deliver(value, c, struct, out, rows):
         block = value * (-col_mask(struct, c))
         out[c] = block
         rows[c % 2, c // 2] = block
 
+    for half in (0, 1):
+        value = za[z, half * 2:(half + 1) * 2]
+        for way in (0, 1):
+            for index in (2, 3):
+                za_copy(way, half, index).wait_recv()
+                value = value + za_in[way, half, index]
+        for c in range(4 * half, 4 * half + 4):
+            deliver(value[c // 2 - 2 * half, c % 2], c, s1, out_a, rows_1)
+    for parity in (0, 1):
+        hand_over(rows_1, ex_a, parity, exa_recv).start()
     all_of(xb_in.at[1:4], xb_recv.at[0])
     value = sb[x] + xb_in[1] + xb_in[2] + xb_in[3]
     for c in range(8):
         deliver(value[c // 2, c % 2], c, s2, out_b, rows_2)
     for parity in (0, 1):
         hand_over(rows_2, ex_b, parity, exb_recv).start()
-    for half in (0, 1):
-        last = [steps_of(way, half) for way in (0, 1)]
-        for way in (0, 1):
-            za_copy(way, half, last[way])[1].wait_recv()
-        value = za[z, half * 2:(half + 1) * 2]
-        value = value + za_in[0, half, last[0] - 1] + za_in[1, half, last[1] - 1]
-        for c in range(4 * half, 4 * half + 4):
-            deliver(value[c // 2 - 2 * half, c % 2], c, s1, out_a, rows_1)
-    for parity in (0, 1):
-        hand_over(rows_1, ex_a, parity, exa_recv).start()
 
     def at_sum(m, j):
         return j * NZ + lax.rem(y + 3 * m, NZ)

time: 90.7 us -> 88 us (0.970)
  Pallas kernels: 81.9 us -> 79.3 us
    pallas_call x1, Pallas kernels: 81.9 us -> 79.3 us  [body(): pl.pallas_call(kernel, out_shape=(rows, square, rows, square, square), in...]
where the time goes in v7:
time: 88 us; the launch traced here: 87.7 us
  Pallas kernels  79.3 us (90%)
  local copies, waits for them, and re-layouts  7.75 us (9%)
    pallas_call x1, Pallas kernels, body(): pl.pallas_call(kernel, out_shape=(rows, square, rows, square, square), in...  79.3 us
    unnamed x5, local copies, waits for them, and re-layouts  7.75 us

profile of v7, /device:TPU:1, one launch (start us, length us, event | category | flops | bytes accessed | tf_op | source)
XLA Modules:
  0.0 87.7 jit_solution(2605329141811655125)
XLA Ops:
  0.6 79.3 %selected_inversion.1 = (f32[8,8,128]{2,1,0:T(8,128)}, f32[256,256]{1,0:T(8,128)}, f32[8,8,128]{2,1,0:T(8,128)}, f32[256,256]{1,0:T(8,128)}, f32[256,256]{1,0:T(8,128)}) custom-call(f32[4096,128]{1,0:T(8,128)} %bitcast.9, f32[4,16,128]{2,1,0:T(8,128)} %bitcast.10, f32[4,16,128]{2,1,0:T(8,128)} %bitcast.11, f32[8,256]{1,0:T(8,128)} %c_hbm.1, ...), custom_call_target="tpu_custom_call" | custom-call | tf_op jit(solution)/shard_map/selected_inversion/pallas_call | solution.py:499
  79.9 1.4 %copy.20 = f32[8,1,8,128]{3,2,1,0:T(8,128)} copy(f32[8,1,8,128]{3,2,1,0:T(8,128)} %bitcast.13) | data formatting | bytes 65536
  81.3 1.7 %copy.21 = f32[256,256]{1,0:T(8,128)} copy(f32[256,256]{1,0:T(8,128)} %get-tuple-element.26) | data formatting | bytes 524288
  82.9 1.4 %copy.22 = f32[8,1,8,128]{3,2,1,0:T(8,128)} copy(f32[8,1,8,128]{3,2,1,0:T(8,128)} %bitcast.12) | data formatting | bytes 65536
  84.3 1.7 %copy.23 = f32[256,256]{1,0:T(8,128)} copy(f32[256,256]{1,0:T(8,128)} %get-tuple-element.28) | data formatting | bytes 524288
  86.0 1.7 %copy.24 = f32[256,256]{1,0:T(8,128)} copy(f32[256,256]{1,0:T(8,128)} %get-tuple-element.29) | data formatting | bytes 524288

commit v8 on v7

--- a/solution.py
+++ b/solution.py
@@ -260,8 +260,9 @@
         )
 
     def zb_step(step):
-        for j in range(4):
+        for i in range(4):
             for way in (0, 1):
+                j = (i + 2 * way) % 4
                 if step > steps_of(way, j // 2):
                     continue
                 d, copy = zb_copy(way, j, step)

time: 88 us -> 88 us (level)
  no operation moved by 1% of the time
where the time goes in v8:
time: 88 us; the launch traced here: 87.6 us
  Pallas kernels  79.2 us (90%)
  local copies, waits for them, and re-layouts  7.75 us (9%)
    pallas_call x1, Pallas kernels, body(): pl.pallas_call(kernel, out_shape=(rows, square, rows, square, square), in...  79.2 us
    unnamed x5, local copies, waits for them, and re-layouts  7.75 us

profile of v8, /device:TPU:1, one launch (start us, length us, event | category | flops | bytes accessed | tf_op | source)
XLA Modules:
  0.0 87.6 jit_solution(3137818030821508829)
XLA Ops:
  0.6 79.2 %selected_inversion.1 = (f32[8,8,128]{2,1,0:T(8,128)}, f32[256,256]{1,0:T(8,128)}, f32[8,8,128]{2,1,0:T(8,128)}, f32[256,256]{1,0:T(8,128)}, f32[256,256]{1,0:T(8,128)}) custom-call(f32[4096,128]{1,0:T(8,128)} %bitcast.9, f32[4,16,128]{2,1,0:T(8,128)} %bitcast.10, f32[4,16,128]{2,1,0:T(8,128)} %bitcast.11, f32[8,256]{1,0:T(8,128)} %c_hbm.1, ...), custom_call_target="tpu_custom_call" | custom-call | tf_op jit(solution)/shard_map/selected_inversion/pallas_call | solution.py:500
  79.9 1.4 %copy.20 = f32[8,1,8,128]{3,2,1,0:T(8,128)} copy(f32[8,1,8,128]{3,2,1,0:T(8,128)} %bitcast.13) | data formatting | bytes 65536
  81.3 1.7 %copy.21 = f32[256,256]{1,0:T(8,128)} copy(f32[256,256]{1,0:T(8,128)} %get-tuple-element.26) | data formatting | bytes 524288
  82.9 1.4 %copy.22 = f32[8,1,8,128]{3,2,1,0:T(8,128)} copy(f32[8,1,8,128]{3,2,1,0:T(8,128)} %bitcast.12) | data formatting | bytes 65536
  84.3 1.7 %copy.23 = f32[256,256]{1,0:T(8,128)} copy(f32[256,256]{1,0:T(8,128)} %get-tuple-element.28) | data formatting | bytes 524288
  86.0 1.7 %copy.24 = f32[256,256]{1,0:T(8,128)} copy(f32[256,256]{1,0:T(8,128)} %get-tuple-element.29) | data formatting | bytes 524288

commit v9 on v7

--- a/solution.py
+++ b/solution.py
@@ -404,17 +404,21 @@
             spot = yz_recv.at[mine]
             pltpu.make_async_copy(tile, place, spot).start()
 
-            def far_first(k):
-                return 4 + (k + 1) // 2 * (1 - 2 * lax.rem(k, 2))
-
-            def spread(k, carry):
-                to_z, to_y = at_z(far_first(k // NY)), at_y(far_first(lax.rem(k, NY)))
-                remote(
-                    tile, place, yz_send.at[0], spot, (x * NZ + to_z, to_y * 2 + core)
-                ).start()
+            far_first = (4, 3, 5, 2, 6, 1, 7, 0)
+            columns = [at_y(k) * 2 + core for k in far_first]
+
+            def spread(to_z, targets):
+                for column in targets:
+                    remote(
+                        tile, place, yz_send.at[0], spot, (x * NZ + to_z, column)
+                    ).start()
+
+            def plane(k, carry):
+                spread(at_z(4 + (k + 1) // 2 * (1 - 2 * lax.rem(k, 2))), columns)
                 return carry
 
-            lax.fori_loop(0, NY * NZ - 1, spread, 0)
+            lax.fori_loop(0, NZ - 1, plane, 0)
+            spread(z, columns[:-1])
 
     make_sums(jnp.logical_or(turn == 0, turn == 3))
     make_sums(turn == 6)

time: 88 us -> 88 us (level)
  no operation moved by 1% of the time
where the time goes in v9:
time: 88 us; the launch traced here: 87.6 us
  Pallas kernels  79.2 us (90%)
  local copies, waits for them, and re-layouts  7.75 us (9%)
    pallas_call x1, Pallas kernels, body(): pl.pallas_call(kernel, out_shape=(rows, square, rows, square, square), in...  79.2 us
    unnamed x5, local copies, waits for them, and re-layouts  7.75 us

profile of v9, /device:TPU:1, one launch (start us, length us, event | category | flops | bytes accessed | tf_op | source)
XLA Modules:
  0.0 87.6 jit_solution(11679292181474556958)
XLA Ops:
  0.6 79.2 %selected_inversion.1 = (f32[8,8,128]{2,1,0:T(8,128)}, f32[256,256]{1,0:T(8,128)}, f32[8,8,128]{2,1,0:T(8,128)}, f32[256,256]{1,0:T(8,128)}, f32[256,256]{1,0:T(8,128)}) custom-call(f32[4096,128]{1,0:T(8,128)} %bitcast.9, f32[4,16,128]{2,1,0:T(8,128)} %bitcast.10, f32[4,16,128]{2,1,0:T(8,128)} %bitcast.11, f32[8,256]{1,0:T(8,128)} %c_hbm.1, ...), custom_call_target="tpu_custom_call" | custom-call | tf_op jit(solution)/shard_map/selected_inversion/pallas_call | solution.py:503
  79.9 1.4 %copy.20 = f32[8,1,8,128]{3,2,1,0:T(8,128)} copy(f32[8,1,8,128]{3,2,1,0:T(8,128)} %bitcast.13) | data formatting | bytes 65536
  81.2 1.7 %copy.21 = f32[256,256]{1,0:T(8,128)} copy(f32[256,256]{1,0:T(8,128)} %get-tuple-element.26) | data formatting | bytes 524288
  82.9 1.4 %copy.22 = f32[8,1,8,128]{3,2,1,0:T(8,128)} copy(f32[8,1,8,128]{3,2,1,0:T(8,128)} %bitcast.12) | data formatting | bytes 65536
  84.3 1.7 %copy.23 = f32[256,256]{1,0:T(8,128)} copy(f32[256,256]{1,0:T(8,128)} %get-tuple-element.28) | data formatting | bytes 524288
  85.9 1.7 %copy.24 = f32[256,256]{1,0:T(8,128)} copy(f32[256,256]{1,0:T(8,128)} %get-tuple-element.29) | data formatting | bytes 524288

commit v10 on v9

--- a/solution.py
+++ b/solution.py
@@ -162,19 +162,19 @@
     across(1, 0)
     got(0, -1)
     got(0, 1)
+    all_of(c_full.at[0:56], cz_recv.at[0])
+    rows64 = pl.ds(pl.multiple_of(x * 64, 64), 64)
+
+    def cx_copy(k):
+        return remote(
+            c_full.at[rows64], c_full.at[rows64], sent.at[0], cx_recv.at[0],
+            (at_x(k) * NZ + z, q),
+        )
+
+    for k in range(1, NX):
+        cx_copy(k).start()
     forward(1, -2)
     forward(1, 2)
-    all_of(c_full.at[0:56], cz_recv.at[0])
-    rows64 = pl.ds(pl.multiple_of(x * 64, 64), 64)
-
-    def cx_copy(k):
-        return remote(
-            c_full.at[rows64], c_full.at[rows64], sent.at[0], cx_recv.at[0],
-            (at_x(k) * NZ + z, q),
-        )
-
-    for k in range(1, NX):
-        cx_copy(k).start()
     got(0, -3)
     got(0, 3)
     got(0, -4)

time: 88 us -> 88 us (level)
  no operation moved by 1% of the time
where the time goes in v10:
time: 88 us; the launch traced here: 87.6 us
  Pallas kernels  79.2 us (90%)
  local copies, waits for them, and re-layouts  7.75 us (9%)
    pallas_call x1, Pallas kernels, body(): pl.pallas_call(kernel, out_shape=(rows, square, rows, square, square), in...  79.2 us
    unnamed x5, local copies, waits for them, and re-layouts  7.75 us

profile of v10, /device:TPU:1, one launch (start us, length us, event | category | flops | bytes accessed | tf_op | source)
XLA Modules:
  0.0 87.6 jit_solution(10052894743039140567)
XLA Ops:
  0.6 79.2 %selected_inversion.1 = (f32[8,8,128]{2,1,0:T(8,128)}, f32[256,256]{1,0:T(8,128)}, f32[8,8,128]{2,1,0:T(8,128)}, f32[256,256]{1,0:T(8,128)}, f32[256,256]{1,0:T(8,128)}) custom-call(f32[4096,128]{1,0:T(8,128)} %bitcast.9, f32[4,16,128]{2,1,0:T(8,128)} %bitcast.10, f32[4,16,128]{2,1,0:T(8,128)} %bitcast.11, f32[8,256]{1,0:T(8,128)} %c_hbm.1, ...), custom_call_target="tpu_custom_call" | custom-call | tf_op jit(solution)/shard_map/selected_inversion/pallas_call | solution.py:503
  79.8 1.4 %copy.20 = f32[8,1,8,128]{3,2,1,0:T(8,128)} copy(f32[8,1,8,128]{3,2,1,0:T(8,128)} %bitcast.13) | data formatting | bytes 65536
  81.2 1.7 %copy.21 = f32[256,256]{1,0:T(8,128)} copy(f32[256,256]{1,0:T(8,128)} %get-tuple-element.26) | data formatting | bytes 524288
  82.9 1.4 %copy.22 = f32[8,1,8,128]{3,2,1,0:T(8,128)} copy(f32[8,1,8,128]{3,2,1,0:T(8,128)} %bitcast.12) | data formatting | bytes 65536
  84.3 1.7 %copy.23 = f32[256,256]{1,0:T(8,128)} copy(f32[256,256]{1,0:T(8,128)} %get-tuple-element.28) | data formatting | bytes 524288
  85.9 1.7 %copy.24 = f32[256,256]{1,0:T(8,128)} copy(f32[256,256]{1,0:T(8,128)} %get-tuple-element.29) | data formatting | bytes 524288
